TPU v7x, 512 devices: a whole 4x8x8 slice. The times are simulated.
512 devices in a mesh: ctx: 16 (over z_hi, y), head: 8 (over x, core), req: 4 (over z_lo).
Axes of the slice: x: 4, y: 8, z: 8 (z_hi: 2, z_lo: 4; z = z_hi * 4 + z_lo), core: 2. Of those that a mesh axis runs over, the one named last changes fastest.
Arguments:
- queries: bfloat16 [16384, 8192], P(('req', 'ctx'), 'head'), parts along dimension 0, may hold values from -5 to 5
- keys: bfloat16 [16384, 1024], P(('req', 'ctx'), 'head'), parts along dimension 0, may hold values from -5 to 5
- values: bfloat16 [16384, 1024], P(('req', 'ctx'), 'head'), parts along dimension 0, may hold values from -6 to 6
- block_order: int32 [128], P('req'), parts along dimension 0, may hold values from 0 to 31, each once
- owner_of: int32 [64], P('req'), parts along dimension 0, may hold values from 0 to 3, as said below
- dec_queries: bfloat16 [16, 128, 8192], P('req', None, 'head'), parts along dimension 0, may hold values from -5 to 5
- dec_pos: int32 [16, 128], P('req'), parts along dimension 0, may hold values from 1 to 4096, as said below
Outputs:
- attn_out: bfloat16 [16384, 8192], P(('req', 'ctx'), 'head'), parts along dimension 0
- owned_keys: bfloat16 [16384, 1024], P(('req', 'ctx'), 'head'), parts along dimension 0
- owned_values: bfloat16 [16384, 1024], P(('req', 'ctx'), 'head'), parts along dimension 0
- dec_out: bfloat16 [16, 128, 8192], P('req', 'ctx', 'head'), parts along dimension 0
There are 4 independent parts, one for each index of `req`. A program takes and returns all parts, laid end to end along the dimension named above; each array names one. Nothing has to cross between parts.
Inputs may be any that keep to these rules, and one draw needn't show every extreme that they name: `owner_of`: each owner group is named by exactly 4 ranks. `dec_pos`: every step has rows that read all 4096 positions and a row that reads one position.
All inputs are finite; a program needn't handle non-finite values.
Results may differ from a plain program's by a relative error of at most 0.023.
Values may be sent and summed in bfloat16 or wider, within the bound.
No kernel may reach another device: no remote copies, remote signals or barrier semaphores. Data moves between devices by JAX's collectives and lax.ppermute only.
A program may use at most 64 MiB of HBM per device.

v0:
```python
import jax
import jax.numpy as jnp
from jax import lax
from jax.sharding import PartitionSpec as P

HD = 128
DROWS = 128
STEPS = 4
OWNERS = 4


LOWEST = -1e30


def block_places(block_order, first_row, count, half):
    index = first_row + jnp.arange(count, dtype=jnp.int32)
    block = index // half
    slots = jnp.arange(block_order.shape[0], dtype=jnp.int32)
    base = jnp.sum(jnp.where(block[:, None] == slots[None, :], block_order[None, :], 0), axis=1)
    return base * half + index % half


def source_rank(owner_of, rank_here, ranks):
    index = jnp.arange(ranks, dtype=jnp.int32)
    same = owner_of[None, :] == owner_of[:, None]
    earlier = index[None, :] < index[:, None]
    before = jnp.sum((same & earlier).astype(jnp.int32), axis=1)
    dest = owner_of * (ranks // OWNERS) + before
    return jnp.sum(jnp.where(dest == rank_here, index, 0))


def partial_scores(query, key_rows, value_rows, visible, state):
    acc, top, total = state
    count = key_rows.shape[0]
    kv_local = query.shape[1]
    scores = jnp.einsum(
        "rkgd,nkd->kgrn",
        query,
        key_rows.reshape(count, kv_local, HD),
        preferred_element_type=jnp.float32,
    ) * HD ** (-0.5)
    scores = jnp.where(visible, scores, LOWEST)
    new_top = jnp.maximum(top, jnp.max(scores, axis=3))
    weights = jnp.where(visible, jnp.exp(scores - new_top[..., None]), 0.0)
    fade = jnp.exp(top - new_top)
    total = total * fade + jnp.sum(weights, axis=3)
    acc = acc * fade[..., None] + jnp.einsum(
        "kgrn,nkd->kgrd",
        weights.astype(jnp.bfloat16),
        value_rows.reshape(count, kv_local, HD),
        preferred_element_type=jnp.float32,
    )
    return (acc, new_top, total)


def per_device(queries, keys, values, block_order, owner_of, dec_queries, dec_pos):
    rows = queries.shape[0]
    half = rows // 2
    kv_local = keys.shape[1] // HD
    group_size = queries.shape[1] // (kv_local * HD)
    ranks = lax.axis_size("ctx")
    rank_here = lax.axis_index("ctx")
    query = queries.reshape(rows, kv_local, group_size, HD)
    query_places = block_places(block_order, rank_here * rows, rows, half)
    source = source_rank(owner_of, rank_here, ranks)

    def visit(state, key_block, value_block, first):
        key_places = block_places(block_order, first, key_block.shape[0], half)
        visible = query_places[:, None] >= key_places[None, :]
        return partial_scores(query, key_block, value_block, visible, state)

    empty_acc = jnp.zeros((kv_local, group_size, rows, HD), jnp.float32)
    empty_top = jnp.full((kv_local, group_size, rows), LOWEST, jnp.float32)
    empty_total = jnp.zeros((kv_local, group_size, rows), jnp.float32)
    start_state = (empty_acc, empty_top, empty_total)
    empty_owned = (jnp.zeros_like(keys), jnp.zeros_like(values))
    key_piece = lax.all_gather(keys, "ctx", axis=0, tiled=True)
    value_piece = lax.all_gather(values, "ctx", axis=0, tiled=True)
    span = key_piece.shape[0]

    def inner(number, carried):
        offset = number * rows
        key_block = lax.dynamic_slice_in_dim(key_piece, offset, rows, 0)
        value_block = lax.dynamic_slice_in_dim(value_piece, offset, rows, 0)
        return visit(carried, key_block, value_block, offset)

    attention = lax.fori_loop(0, span // rows, inner, start_state)
    capture_key_piece = lax.all_gather(keys, "ctx", axis=0, tiled=True)
    capture_value_piece = lax.all_gather(values, "ctx", axis=0, tiled=True)
    span = capture_key_piece.shape[0]
    wanted = jnp.arange(rows, dtype=jnp.int32) + source * rows
    valid = (wanted >= 0) & (wanted < span)
    picked = jnp.clip(wanted, 0, span - 1)
    owned = (
        jnp.where(valid[:, None], capture_key_piece[picked], empty_owned[0]),
        jnp.where(valid[:, None], capture_value_piece[picked], empty_owned[1]),
    )
    acc, top, total = attention
    mixed = acc / total[..., None]
    attn_out = jnp.transpose(mixed, (2, 0, 1, 3)).reshape(rows, kv_local * group_size * HD)
    owned_keys, owned_values = owned
    cache_places = block_places(block_order, source * rows, rows, half)
    dec_rows = STEPS * DROWS
    dec_query = dec_queries.reshape(dec_rows, kv_local, group_size, HD)
    limits = dec_pos.reshape(dec_rows)
    dec_visible = cache_places[None, :] < limits[:, None]
    dec_scores = jnp.einsum(
        "rkgd,nkd->kgrn",
        dec_query,
        owned_keys.reshape(rows, kv_local, HD),
        preferred_element_type=jnp.float32,
    ) * HD ** (-0.5)
    dec_scores = jnp.where(dec_visible, dec_scores, LOWEST)
    local_top = jnp.max(dec_scores, axis=3)
    whole_top = lax.pmax(local_top, "ctx")
    dec_weights = jnp.where(dec_visible, jnp.exp(dec_scores - whole_top[..., None]), 0.0)
    dec_total = jnp.sum(dec_weights, axis=3)
    dec_acc = jnp.einsum(
        "kgrn,nkd->kgrd",
        dec_weights.astype(jnp.bfloat16),
        owned_values.reshape(rows, kv_local, HD),
        preferred_element_type=jnp.float32,
    )
    part_acc = lax.optimization_barrier(dec_acc.astype(jnp.bfloat16)).astype(jnp.float32)
    part_total = lax.optimization_barrier(dec_total.astype(jnp.bfloat16)).astype(jnp.float32)
    part_acc = part_acc.reshape(kv_local, group_size, STEPS, DROWS, HD)
    part_total = part_total.reshape(kv_local, group_size, STEPS, DROWS)
    share = DROWS // ranks
    whole_acc, whole_total = (
        lax.psum(part_acc.astype(jnp.bfloat16), "ctx").astype(jnp.float32),
        lax.psum(part_total.astype(jnp.bfloat16), "ctx").astype(jnp.float32),
    )
    mine_acc = lax.dynamic_slice_in_dim(whole_acc, rank_here * share, share, 3)
    mine_total = lax.dynamic_slice_in_dim(whole_total, rank_here * share, share, 3)
    dec_mixed = mine_acc / mine_total[..., None]
    dec_out = jnp.transpose(dec_mixed, (2, 3, 0, 1, 4)).reshape(
        STEPS, share, kv_local * group_size * HD
    )
    return (attn_out.astype(jnp.bfloat16), owned_keys, owned_values, dec_out.astype(jnp.bfloat16))


def solution(mesh):
    placed = (
        P(("req", "ctx"), "head"),
        P(("req", "ctx"), "head"),
        P(("req", "ctx"), "head"),
        P("req"),
        P("req"),
        P("req", None, "head"),
        P("req", None),
    )
    return jax.shard_map(
        per_device,
        mesh=mesh,
        in_specs=placed,
        out_specs=(
            P(("req", "ctx"), "head"),
            P(("req", "ctx"), "head"),
            P(("req", "ctx"), "head"),
            P("req", "ctx", "head"),
        ),
        check_vma=False,
    )
```

profile of v0, /device:TPU:6, one launch (start us, length us, event | category | flops | bytes accessed | tf_op | source)
XLA Modules:
  0.0 417.3 jit_solution(8665660019011947057)
XLA Ops:
  8.7 0.9 convert_reduce_fusion
  9.7 1.3 fusion.57
  11.6 1.3 copy.24
  13.8 95.4 %all-gather.3.cloned.1.call-done = bf16[4096,128]{1,0:T(8,128)(2,1)} async-done(((bf16[256,128]{1,0:T(8,128)(2,1)}), bf16[4096,128]{1,0:T(8,128)(2,1)}) %all-gather.3.cloned.1.call-update) | async-done | bytes 1048592 | tf_op jit(solution)/shard_map/all_gather | solution.py:77
  109.2 2.1 gather_fusion
  111.3 2.9 fusion.25
  114.2 92.1 %pmax.7 = f32[8,512]{1,0:T(8,128)S(1)} all-reduce(f32[8,512]{1,0:T(8,128)S(1)} %get-tuple-element.304), channel_id=1, replica_groups=mesh['ctx'=16,'head'=8,'req'=4] {'ctx'}, use_global_device_ids=true, to_apply=%region_10.11 | all-reduce | flops 4096 | bytes 32768 | tf_op jit(solution)/shard_map/pmax | solution.py:115
  206.2 2.1 gather_fusion.1
  208.3 4.8 %fusion.39 = bf16[1,8,512,128]{3,2,1,0:T(8,128)(2,1)} fusion(f32[256,512,8]{1,0,2:T(8,128)} %get-tuple-element.305, f32[8,512]{1,0:T(8,128)S(1)} %pmax.7, pred[512,256]{0,1:T(8,128)(4,1)S(1)} %broadcast_compare_fusion.2, bf16[256,128]{1,0:T(8,128)(2,1)S(1)} %gather_fusion.1, pred[256]{0:T(512)(128)(4,1)S(1)} %compare_and_fusion), kind=kOutput, calls=%fused_computation.57 | convolution fusion | flops 274235392 | bytes 5456128 | tf_op jit(solution)/shard_map/kgrn,nkd->kgrd/dot_general | solution.py:118
  213.1 85.1 %while.20 = (s32[]{:T(128)}, f32[1,8,256,128]{3,2,1,0:T(8,128)}, f32[1,8,256]{2,1,0:T(8,128)S(1)}, f32[1,8,256]{2,1,0:T(8,128)S(1)}, s32[256]{0:T(256)S(1)}, /*i...) while((s32[]{:T(128)}, f32[1,8,256,128]{3,2,1,0:T(8,128)}, ...), condition=%wide.region_5.6_spmd.clone, body=%wide.region_1.5_spmd.clone.sunk | while | flops 276147456 | bytes 9444687 | solution.py:87
  213.4 1.3 fusion.74
  214.7 2.8 fusion.76
  218.3 1.3 fusion.74
  219.6 3.2 fusion.76
  223.6 1.3 fusion.74
  225.0 3.2 fusion.76
  229.0 1.3 fusion.74
  230.3 3.2 fusion.76
  234.3 1.3 fusion.74
  235.7 3.2 fusion.76
  239.7 1.3 fusion.74
  241.0 3.2 fusion.76
  245.0 1.3 fusion.74
  246.4 3.2 fusion.76
  250.4 1.3 fusion.74
  251.7 3.2 fusion.76
  255.7 1.3 fusion.74
  257.1 3.2 fusion.76
  261.1 1.3 fusion.74
  262.4 3.2 fusion.76
  266.4 1.3 fusion.74
  267.8 3.2 fusion.76
  271.8 1.3 fusion.74
  273.1 3.2 fusion.76
  277.1 1.3 fusion.74
  278.4 3.2 fusion.76
  282.5 1.3 fusion.74
  283.8 3.2 fusion.76
  287.8 1.3 fusion.74
  289.1 3.2 fusion.76
  293.2 1.3 fusion.74
  294.5 3.2 fusion.76
  298.2 1.6 fusion.44
  300.2 0.9 copy.40
  301.1 3.2 fusion.26
  304.3 46.9 %psum.15 = bf16[1,8,4,128]{3,2,1,0:T(4,128)(2,1)S(1)} all-reduce(bf16[1,8,4,128]{3,2,1,0:T(4,128)(2,1)S(1)} %convert_element_type.97), channel_id=1, replica_groups=mesh['ctx'=16,'head'=8,'req'=4] {'ctx'}, use_global_device_ids=true, to_apply=%region_13.14 | all-reduce | flops 4096 | bytes 16384 | tf_op jit(solution)/shard_map/psum | solution.py:131
  352.0 57.1 %all-reduce.2.cloned.1.call-done = bf16[1,8,4,128,128]{4,3,2,1,0:T(8,128)(2,1)} async-done(((bf16[1,8,4,128,128]{4,3,2,1,0:T(8,128)(2,1)}), bf16[1,8,4,128,128]{4,3,2,1,0:T(8,128)(2,1)}) %all-reduce.2.cloned.1.call-update) | async-done | bytes 1048592 | tf_op jit(solution)/shard_map/psum | solution.py:130
  409.2 1.6 copy_bitcast_fusion.1
  (158 shorter events, 15.7 us)
Async XLA Ops:
  7.2 6.0 %copy-start = (bf16[4,128,1024]{2,1,0:T(8,128)(2,1)S(1)}, bf16[4,128,1024]{2,1,0:T(8,128)(2,1)}, u32[]{:S(2)}) copy-start(bf16[4,128,1024]{2,1,0:T(8,128)(2,1)} %param.14) | copy-start | bytes 3145732
  7.2 102.0 %all-gather.3.cloned.1.call-start = ((), (), s32[]{:S(2)}) async-start(), calls=%async_computation | async-start | bytes 1114112 | tf_op jit(solution)/shard_map/all_gather | solution.py:77
  7.9 198.3 %all-gather.5.cloned.1.call-start = ((), (), s32[]{:S(2)}) async-start(), calls=%async_computation.1 | async-start | bytes 1114112 | tf_op jit(solution)/shard_map/all_gather | solution.py:78
  8.7 400.5 %all-reduce.2.cloned.1.call-start = ((), (), s32[]{:S(2)}) async-start(), calls=%async_computation.2 | async-start | bytes 2097152 | tf_op jit(solution)/shard_map/psum | solution.py:130
  11.6 1.9 copy-start.1
  11.6 2.0 copy-start.2
Sparse Core Ops, SparseCore 0:
  11.2 97.9 all-gather.2
  112.4 86.9 all-gather.4
  213.2 195.8 all-reduce.1
where the time goes:
time: 419 us; the launch traced here: 417 us
  waiting for transfers between devices  154 us (37%)
  blocking collectives  139 us (33%)
  matrix products  79.4 us (19%)
  other arithmetic  21.8 us (5%)
  between operations  14.6 us (3%)
  local copies, waits for them, and re-layouts  7.27 us (2%)
    all_gather x1, waiting for transfers between devices, per_device(): key_piece = lax.all_gather(keys, 'ctx', axis=0, tiled=True)  95.4 us
    pmax x1, blocking collectives, per_device(): whole_top = lax.pmax(local_top, 'ctx')  92.1 us
    psum x1, waiting for transfers between devices, per_device(): lax.psum(part_acc.astype(jnp.bfloat16), 'ctx').astype(jnp.float32)  57.1 us
    dot_general x16, matrix products, partial_scores(): jnp.einsum('kgrn,nkd->kgrd', weights.astype(jnp.bfloat16), value_rows.res...  50.9 us
    psum x1, blocking collectives, per_device(): lax.psum(part_total.astype(jnp.bfloat16), 'ctx').astype(jnp.float32)  46.9 us
    dot_general x16, matrix products, partial_scores(): jnp.einsum('rkgd,nkd->kgrn', query, key_rows.reshape(count, kv_local, HD)...  20.9 us
  transfers between devices with their start and end apart: 3, of which 2 were waited for; matrix products, arithmetic and copies ran while one was open for 24% of the time, Pallas kernels for 0%

commit v1 on v0

v1 whole, which is shorter than its diff:
```python
import functools

import jax
import jax.numpy as jnp
from jax import lax
from jax.experimental import pallas as pl
from jax.experimental.pallas import tpu as pltpu
from jax.sharding import PartitionSpec as P

HD = 128
BLK = 128
DROWS = 128
STEPS = 4
OWNERS = 4
HALVES = 2

LOWEST = -1e30
LOG2E = 1.4426950408889634
SCALE = LOG2E * HD ** (-0.5)
CHUNK = 512


def source_rank(owner_of, rank_here, ranks):
    index = jnp.arange(ranks, dtype=jnp.int32)
    same = owner_of[None, :] == owner_of[:, None]
    earlier = index[None, :] < index[:, None]
    before = jnp.sum((same & earlier).astype(jnp.int32), axis=1)
    dest = owner_of * (ranks // OWNERS) + before
    return jnp.sum(jnp.where(dest == rank_here, index, 0))


def attend(query, pairs, key_places, row_places, acc, total, top):
    count = pairs.shape[0]
    for first in range(0, count, CHUNK):
        width = min(CHUNK, count - first)
        key_rows = pairs[first : first + width, 0:HD]
        value_rows = pairs[first : first + width, HD : 2 * HD]
        places = key_places[:, first : first + width]
        scores = lax.dot_general(
            query, key_rows, (((1,), (1,)), ((), ())), preferred_element_type=jnp.float32
        )
        visible = jnp.tile(row_places, (1, width // HD)) >= places
        scores = jnp.where(visible, scores, LOWEST)
        new_top = jnp.maximum(top, jnp.max(scores, axis=1, keepdims=True))
        weights = jnp.exp2(scores * SCALE - jnp.tile(new_top * SCALE, (1, width // HD)))
        fade = jnp.exp2((top - new_top) * SCALE)
        wide = jnp.concatenate([value_rows, jnp.ones_like(value_rows)], axis=1)
        mixed = jnp.dot(weights.astype(jnp.bfloat16), wide, preferred_element_type=jnp.float32)
        acc = acc * fade + mixed[:, 0:HD]
        total = total * fade + mixed[:, HD : 2 * HD]
        top = new_top
    return acc, total, top


def group_query(group, heads, query_ref, dec_query_ref):
    return jnp.where(group < heads, query_ref[...], dec_query_ref[...])


def first_kernel(heads, query_ref, dec_query_ref, pairs_ref, key_places_ref, row_places_ref, state_ref):
    group = pl.program_id(0)
    query = group_query(group, heads, query_ref, dec_query_ref)
    rows = query.shape[0]
    acc = jnp.zeros((rows, HD), jnp.float32)
    top = jnp.full((rows, HD), LOWEST, jnp.float32)
    acc, total, top = attend(query, pairs_ref, key_places_ref[...], row_places_ref[0], acc, acc, top)
    lane = lax.broadcasted_iota(jnp.int32, (rows, HD), 1)
    state_ref[0, :, 0:HD] = acc
    state_ref[0, :, HD : 2 * HD] = jnp.where(lane < HD // 2, total, top)


def last_kernel(
    heads,
    pick_ref,
    query_ref,
    dec_query_ref,
    pairs_ref,
    key_places_ref,
    row_places_ref,
    state_ref,
    other_ref,
    out_ref,
    owned_keys_ref,
    owned_values_ref,
    dec_out_ref,
):
    group = pl.program_id(0)
    query = group_query(group, heads, query_ref, dec_query_ref)
    rows = query.shape[0]
    acc = state_ref[0, :, 0:HD]
    total = jnp.broadcast_to(state_ref[0, :, HD : HD + 1], (rows, HD))
    top = jnp.broadcast_to(state_ref[0, :, 2 * HD - 1 : 2 * HD], (rows, HD))
    acc, total, top = attend(query, pairs_ref, key_places_ref[...], row_places_ref[0], acc, total, top)
    mixed = (acc / total).astype(out_ref.dtype)

    @pl.when(group == 0)
    def _():
        here = pairs_ref[pl.ds(pl.multiple_of(pick_ref[1], rows), rows), :]
        picked = jnp.where(pick_ref[0] == 1, here, other_ref[...])
        owned_keys_ref[...] = picked[:, 0:HD]
        owned_values_ref[...] = picked[:, HD : 2 * HD]

    @pl.when(group < heads)
    def _():
        out_ref[...] = mixed

    @pl.when(group == heads)
    def _():
        steps, share = dec_out_ref.shape[0], dec_out_ref.shape[1]
        for head in range(heads):
            piece = mixed[head * steps * share : (head + 1) * steps * share]
            dec_out_ref[:, :, head * HD : (head + 1) * HD] = piece.reshape(steps, share, HD)


def per_device(queries, keys, values, block_order, owner_of, dec_queries, dec_pos):
    rows = queries.shape[0]
    heads = queries.shape[1] // HD
    groups = heads + 1
    ranks = lax.axis_size("ctx")
    rank_here = lax.axis_index("ctx")
    along = ranks // HALVES
    half_here = rank_here // along
    lines = [[half * along + place for place in range(along)] for half in range(HALVES)]
    swap = [(rank, (rank + along) % ranks) for rank in range(ranks)]
    share = DROWS // ranks

    pair = jnp.concatenate([keys, values], axis=1)
    near = lax.all_gather(pair, "ctx", axis=0, axis_index_groups=lines, tiled=True)
    partner = lax.ppermute(pair, "ctx", swap)
    copies = jnp.broadcast_to(partner[None], (along,) + partner.shape)
    far = lax.all_to_all(copies, "ctx", 0, 0, axis_index_groups=lines)
    far = far.reshape(along * rows, 2 * HD)

    places = (block_order[:, None] * BLK + jnp.arange(BLK, dtype=jnp.int32)[None, :]).reshape(1, -1)
    span = along * rows
    near_places = lax.dynamic_slice_in_dim(places, half_here * span, span, 1)
    far_places = lax.dynamic_slice_in_dim(places, (1 - half_here) * span, span, 1)
    query_places = lax.dynamic_slice_in_dim(places, rank_here * rows, rows, 1).reshape(rows)
    dec_mine = lax.dynamic_slice_in_dim(dec_queries, rank_here * share, share, 1)
    dec_query = jnp.transpose(dec_mine.reshape(STEPS * share, heads, HD), (1, 0, 2)).reshape(-1, HD)
    limits = lax.dynamic_slice_in_dim(dec_pos, rank_here * share, share, 1).reshape(-1)
    dec_places = jnp.tile(limits - 1, (heads,))
    row_places = jnp.stack([query_places, dec_places])
    row_places = jnp.broadcast_to(row_places[:, :, None], (2, rows, HD))

    source = source_rank(owner_of, rank_here, ranks)
    source_near = source // along == half_here
    offset = (source % along) * rows
    other = lax.dynamic_slice_in_dim(far, offset, rows, 0)
    pick = jnp.stack([source_near.astype(jnp.int32), offset])

    whole = lambda *shape: pl.BlockSpec(shape, lambda group, *_: (0,) * len(shape))
    query_spec = pl.BlockSpec((rows, HD), lambda group, *_: (0, jnp.minimum(group, heads - 1)))
    places_spec = pl.BlockSpec((1, rows, HD), lambda group, *_: (group // heads, 0, 0))
    state_spec = pl.BlockSpec((1, rows, 2 * HD), lambda group, *_: (group, 0, 0))
    params = pltpu.CompilerParams(vmem_limit_bytes=48 * 2**20)
    inputs = [query_spec, whole(rows, HD), whole(span, 2 * HD), whole(1, span), places_spec]
    cost = pl.CostEstimate(
        flops=4 * groups * rows * span * HD,
        bytes_accessed=groups * rows * HD * 12 + span * HD * 4,
        transcendentals=groups * rows * span,
    )
    state = pl.pallas_call(
        functools.partial(first_kernel, heads),
        grid=(groups,),
        in_specs=inputs,
        out_specs=state_spec,
        out_shape=jax.ShapeDtypeStruct((groups, rows, 2 * HD), jnp.float32),
        compiler_params=params,
        cost_estimate=cost,
        name="attend_far",
    )(queries, dec_query, far, far_places, row_places)
    return pl.pallas_call(
        functools.partial(last_kernel, heads),
        grid_spec=pltpu.PrefetchScalarGridSpec(
            num_scalar_prefetch=1,
            grid=(groups,),
            in_specs=inputs + [state_spec, whole(rows, 2 * HD)],
            out_specs=[
                query_spec,
                whole(rows, HD),
                whole(rows, HD),
                whole(STEPS, share, heads * HD),
            ],
        ),
        out_shape=[
            jax.ShapeDtypeStruct(queries.shape, queries.dtype),
            jax.ShapeDtypeStruct(keys.shape, keys.dtype),
            jax.ShapeDtypeStruct(values.shape, values.dtype),
            jax.ShapeDtypeStruct((STEPS, share, heads * HD), queries.dtype),
        ],
        compiler_params=params,
        cost_estimate=cost,
        name="attend_near",
    )(pick, queries, dec_query, near, near_places, row_places, state, other)


def solution(mesh):
    placed = (
        P(("req", "ctx"), "head"),
        P(("req", "ctx"), "head"),
        P(("req", "ctx"), "head"),
        P("req"),
        P("req"),
        P("req", None, "head"),
        P("req", None),
    )
    return jax.shard_map(
        per_device,
        mesh=mesh,
        in_specs=placed,
        out_specs=(
            P(("req", "ctx"), "head"),
            P(("req", "ctx"), "head"),
            P(("req", "ctx"), "head"),
            P("req", "ctx", "head"),
        ),
        check_vma=False,
    )
```

time: 419 us -> 105 us (0.25)
  blocking collectives: 139 us -> 0 us
  waiting for transfers between devices: 154 us -> 37.4 us
  matrix products: 79.4 us -> 0 us
  Pallas kernels: 0 us -> 23.2 us
  other arithmetic: 21.8 us -> 1.06 us
  starting transfers between devices: 0.11 us -> 18.1 us
    pmax x1 -> x0, blocking collectives: 92.1 us -> none  [per_device(): whole_top = lax.pmax(local_top, 'ctx')]
    all_gather x2 -> x1, waiting for transfers between devices: 95.4 us -> 9.94 us  [per_device(): lax.all_gather(pair, 'ctx', axis=0, axis_index_groups=lines, tiled=True)]
    dot_general x34 -> x0, matrix products: 79.4 us -> none  [the longest x16 50.9 us: partial_scores(): jnp.einsum('kgrn,nkd->kgrd', weights.astype(jnp.bfloat16), value_rows.res...]
    psum x1 -> x0, waiting for transfers between devices: 57.1 us -> none  [per_device(): lax.psum(part_acc.astype(jnp.bfloat16), 'ctx').astype(jnp.float32)]
    psum x1 -> x0, blocking collectives: 46.9 us -> none  [per_device(): lax.psum(part_total.astype(jnp.bfloat16), 'ctx').astype(jnp.float32)]
    all_to_all x0 -> x1, waiting for transfers between devices: none -> 23.2 us  [per_device(): far = lax.all_to_all(copies, 'ctx', 0, 0, axis_index_groups=lines)]
    pallas_call x0 -> x2, Pallas kernels: none -> 23.2 us  [the longest x1 12.8 us: per_device(): pl.pallas_call(functools.partial(last_kernel, heads), grid_spec=pltpu.Pre...]
    reduce_sum x34 -> x0, other arithmetic: 13 us -> none  [the longest x16 8.23 us: partial_scores(): total = total * fade + jnp.sum(weights, axis=3)]
  transfers between devices with their start and end apart: 3 -> 3, of which waited for: 2 -> 3; matrix products, arithmetic and copies ran while one was open for 24% -> 1% of each run, Pallas kernels for 0% -> 10%
where the time goes in v1:
time: 105 us; the launch traced here: 104 us
  waiting for transfers between devices  37.4 us (36%)
  Pallas kernels  23.2 us (22%)
  starting transfers between devices  18.1 us (17%)
  between operations  16.9 us (16%)
  local copies, waits for them, and re-layouts  7.56 us (7%)
  other arithmetic  1.06 us (1%)
    all_to_all x1, waiting for transfers between devices, per_device(): far = lax.all_to_all(copies, 'ctx', 0, 0, axis_index_groups=lines)  23.2 us
    pallas_call x1, Pallas kernels, per_device(): pl.pallas_call(functools.partial(last_kernel, heads), grid_spec=pltpu.Pre...  12.8 us
    ppermute x1, starting transfers between devices, per_device(): partner = lax.ppermute(pair, 'ctx', swap)  10.9 us
    pallas_call x1, Pallas kernels, per_device(): pl.pallas_call(functools.partial(first_kernel, heads), grid=(groups,), in...  10.4 us
    all_gather x1, waiting for transfers between devices, per_device(): lax.all_gather(pair, 'ctx', axis=0, axis_index_groups=lines, tiled=True)  9.94 us
    all_to_all x1, starting transfers between devices, per_device(): far = lax.all_to_all(copies, 'ctx', 0, 0, axis_index_groups=lines)  7.1 us
    unnamed x21, local copies, waits for them, and re-layouts  5.28 us
    ppermute x1, waiting for transfers between devices, per_device(): partner = lax.ppermute(pair, 'ctx', swap)  3.58 us
  transfers between devices with their start and end apart: 3, of which 3 were waited for; matrix products, arithmetic and copies ran while one was open for 1% of the time, Pallas kernels for 10%

profile of v1, /device:TPU:6, one launch (start us, length us, event | category | flops | bytes accessed | tf_op | source)
XLA Modules:
  0.0 104.1 jit_solution(12723855701150559804)
XLA Ops:
  7.2 0.0 copy-start
  7.2 0.0 copy-start.7
  7.2 0.0 copy-start.6
  7.2 0.0 copy-start.8
  7.2 0.9 constant_dynamic-update-slice_fusion.1
  8.1 0.0 copy-start.2
  8.2 0.9 constant_dynamic-update-slice_fusion
  9.1 0.0 copy-start.5
  9.1 10.9 %collective-permute-start = (bf16[256,256]{1,0:T(8,128)(2,1)S(1)}, bf16[256,256]{1,0:T(8,128)(2,1)S(1)}, u32[]{:S(2)}, u32[]{:S(2)}) collective-permute-start(bf16[256,256]{1,0:T(8,128)(2,1)S(1)} %constant_dynamic-update-slice_fusion), channel_id=1, source_target_pairs={{0,256},{32,288},{64,320},{96,352},{128,384},{160,416},{192,448},{... | collective-permute-start | bytes 393224 | tf_op jit(solution)/shard_map/ppermute | solution.py:128
  20.0 3.6 %collective-permute-done = bf16[256,256]{1,0:T(8,128)(2,1)S(1)} collective-permute-done((bf16[256,256]{1,0:T(8,128)(2,1)S(1)}, bf16[256,256]{1,0:T(8,128)(2,1)S(1)}, u32[]{:S(2)}, u32[]{:S(2)}) %collective-permute-start) | collective-permute-done | bytes 131104 | tf_op jit(solution)/shard_map/ppermute | solution.py:128
  23.6 1.0 %broadcast_in_dim.9 = bf16[8,256,256]{2,1,0:T(8,128)(2,1)} broadcast(bf16[256,256]{1,0:T(8,128)(2,1)S(1)} %collective-permute-done), dimensions={1,2} | broadcast | bytes 1179648 | tf_op jit(solution)/shard_map/broadcast_in_dim | solution.py:129
  24.6 7.1 %all-to-all-start = ((bf16[8,256,256]{2,1,0:T(8,128)(2,1)}), bf16[8,256,256]{2,1,0:T(8,128)(2,1)S(1)}, u32[]{:S(2)}, u32[]{:S(2)}) async-start(bf16[8,256,256]{2,1,0:T(8,128)(2,1)} %broadcast_in_dim.9), calls=%async_computation | async-start | bytes 2097152 | tf_op jit(solution)/shard_map/all_to_all | solution.py:130
  31.7 0.0 all-gather.2.cloned.1.call-start
  31.8 0.0 copy-done.5
  31.8 0.7 all-gather.2.cloned.1.call-update
  32.5 0.0 copy-done.7
  32.5 0.2 convert_reduce_fusion
  32.7 0.6 fusion.1
  35.9 0.0 copy-done.6
  35.9 0.1 dynamic-slice_add_fusion
  36.0 0.1 sub.19
  36.1 0.1 stack_tile.3
  36.2 0.0 copy-done
  36.3 0.1 pad_add_fusion.1.pick_ref
  36.4 0.0 copy-done.8
  36.4 0.1 iota_add_fusion
  36.5 23.2 %all-to-all-done = bf16[8,256,256]{2,1,0:T(8,128)(2,1)S(1)} async-done(((bf16[8,256,256]{2,1,0:T(8,128)(2,1)}), bf16[8,256,256]{2,1,0:T(8,128)(2,1)S(1)}, u32[]{:S(2)}, u32[]{:S(2)}) %all-to-all-start) | async-done | bytes 1048608 | tf_op jit(solution)/shard_map/all_to_all | solution.py:130
  59.7 0.1 broadcast_in_dim.8.row_places_ref
  59.8 0.0 copy-done.2
  59.8 10.4 %attend_far.1.state_ref = f32[9,256,256]{2,1,0:T(8,128)S(1)} custom-call(bf16[256,1024]{1,0:T(8,128)(2,1)S(1)} %copy-done.2, bf16[256,128]{1,0:T(8,128)(2,1)S(1)} %bitcast.13, bf16[2048,256]{1,0:T(8,128)(2,1)S(1)} %bitcast.12, s32[1,2048]{1,0:T(1,128)S(1)} %get-tuple-element.4.key_places_ref, s32[2,256,128]{2,1,0:T(8,128)S(1)} %broadcast_in_dim.8.row_places_ref), custom_call_target="tpu_custom_call" | custom-call | flops 2415919104 | bytes 4587520 | tf_op jit(solution)/shard_map/attend_far/pallas_call | solution.py:162
  70.2 0.0 copy-start.3
  70.2 1.4 %copy-done.3 = f32[9,256,256]{2,1,0:T(8,128)} copy-done((f32[9,256,256]{2,1,0:T(8,128)}, f32[9,256,256]{2,1,0:T(8,128)S(1)}, u32[]{:S(2)}) %copy-start.3) | copy-done | bytes 2359320
  71.6 9.9 %all-gather.2.cloned.1.call-done.pairs_ref = bf16[2048,256]{1,0:T(8,128)(2,1)} async-done(((bf16[256,256]{1,0:T(8,128)(2,1)}), bf16[2048,256]{1,0:T(8,128)(2,1)}) %all-gather.2.cloned.1.call-update) | async-done | bytes 1048592 | tf_op jit(solution)/shard_map/all_gather | solution.py:127
  81.6 0.0 copy-start.1
  81.6 1.2 %copy-done.1 = bf16[2048,256]{1,0:T(8,128)(2,1)S(1)} copy-done((bf16[2048,256]{1,0:T(8,128)(2,1)S(1)}, bf16[2048,256]{1,0:T(8,128)(2,1)}, u32[]{:S(2)}) %copy-start.1) | copy-done | bytes 1048600
  82.8 0.0 copy-start.4
  82.8 1.7 %copy-done.4 = f32[9,256,256]{2,1,0:T(8,128)S(1)} copy-done((f32[9,256,256]{2,1,0:T(8,128)S(1)}, f32[9,256,256]{2,1,0:T(8,128)}, u32[]{:S(2)}) %copy-start.4) | copy-done | bytes 2359320
  84.5 12.8 %attend_near.1 = (bf16[256,1024]{1,0:T(8,128)(2,1)}, bf16[256,128]{1,0:T(8,128)(2,1)}, bf16[256,128]{1,0:T(8,128)(2,1)}, bf16[4,8,1024]{2,1,0:T(8,128)(2,1)}) custom-call(s32[2]{0:T(128)S(1)} %pad_add_fusion.1.pick_ref, bf16[256,1024]{1,0:T(8,128)(2,1)S(1)} %copy-done.2, bf16[256,128]{1,0:T(8,128)(2,1)S(1)} %bitcast.14, bf16[2048,256]{1,0:T(8,128)(2,1)S(1)} %copy-done.1, ...), custom_call_target="tpu_custom_call" | custom-call | flops 2415919104 | bytes 4587520 | tf_op jit(solution)/shard_map/attend_near/pallas_call | solution.py:172
  (9 shorter events, 0.1 us)
Async XLA Ops:
  7.2 29.0 %copy-start = (bf16[4,128,1024]{2,1,0:T(8,128)(2,1)S(1)}, bf16[4,128,1024]{2,1,0:T(8,128)(2,1)}, u32[]{:S(2)}) copy-start(bf16[4,128,1024]{2,1,0:T(8,128)(2,1)} %param.12) | copy-start | bytes 3145732
  7.2 25.3 %copy-start.7 = (s32[16]{0:T(128)S(1)}, s32[16]{0:T(128)}, u32[]{:S(2)}) copy-start(s32[16]{0:T(128)} %param.11) | copy-start | bytes 196
  7.2 28.8 %copy-start.6 = (s32[4,128]{1,0:T(4,128)S(1)}, s32[4,128]{1,0:T(4,128)}, u32[]{:S(2)}) copy-start(s32[4,128]{1,0:T(4,128)} %param.13) | copy-start | bytes 6148
  7.2 29.2 %copy-start.8 = (s32[32]{0:T(128)S(1)}, s32[32]{0:T(128)}, u32[]{:S(2)}) copy-start(s32[32]{0:T(128)} %param.10) | copy-start | bytes 388
  8.1 51.7 %copy-start.2 = (bf16[256,1024]{1,0:T(8,128)(2,1)S(1)}, bf16[256,1024]{1,0:T(8,128)(2,1)}, u32[]{:S(2)}) copy-start(bf16[256,1024]{1,0:T(8,128)(2,1)} %query_ref.3) | copy-start | bytes 1572868
  9.1 22.7 %copy-start.5 = (bf16[256,256]{1,0:T(8,128)(2,1)}, bf16[256,256]{1,0:T(8,128)(2,1)S(1)}, u32[]{:S(2)}) copy-start(bf16[256,256]{1,0:T(8,128)(2,1)S(1)} %constant_dynamic-update-slice_fusion) | copy-start | bytes 393220
  9.1 14.5 %collective-permute-start = (bf16[256,256]{1,0:T(8,128)(2,1)S(1)}, bf16[256,256]{1,0:T(8,128)(2,1)S(1)}, u32[]{:S(2)}, u32[]{:S(2)}) collective-permute-start(bf16[256,256]{1,0:T(8,128)(2,1)S(1)} %constant_dynamic-update-slice_fusion), channel_id=1, source_target_pairs={{0,256},{32,288},{64,320},{96,352},{128,384},{160,416},{192,448},{... | collective-permute-start | bytes 393224 | tf_op jit(solution)/shard_map/ppermute | solution.py:128
  24.6 35.1 %all-to-all-start = ((bf16[8,256,256]{2,1,0:T(8,128)(2,1)}), bf16[8,256,256]{2,1,0:T(8,128)(2,1)S(1)}, u32[]{:S(2)}, u32[]{:S(2)}) async-start(bf16[8,256,256]{2,1,0:T(8,128)(2,1)} %broadcast_in_dim.9), calls=%async_computation | async-start | bytes 2097152 | tf_op jit(solution)/shard_map/all_to_all | solution.py:130
  31.7 49.8 %all-gather.2.cloned.1.call-start = ((), (), s32[]{:S(2)}) async-start(), calls=%async_computation.1 | async-start | bytes 1179648 | tf_op jit(solution)/shard_map/all_gather | solution.py:127
  70.2 1.4 %copy-start.3 = (f32[9,256,256]{2,1,0:T(8,128)}, f32[9,256,256]{2,1,0:T(8,128)S(1)}, u32[]{:S(2)}) copy-start(f32[9,256,256]{2,1,0:T(8,128)S(1)} %attend_far.1.state_ref) | copy-start | bytes 7077892
  81.6 1.2 %copy-start.1 = (bf16[2048,256]{1,0:T(8,128)(2,1)S(1)}, bf16[2048,256]{1,0:T(8,128)(2,1)}, u32[]{:S(2)}) copy-start(bf16[2048,256]{1,0:T(8,128)(2,1)} %all-gather.2.cloned.1.call-done.pairs_ref) | copy-start | bytes 3145732
  82.8 1.7 %copy-start.4 = (f32[9,256,256]{2,1,0:T(8,128)S(1)}, f32[9,256,256]{2,1,0:T(8,128)}, u32[]{:S(2)}) copy-start(f32[9,256,256]{2,1,0:T(8,128)} %copy-done.3) | copy-start | bytes 7077892
Sparse Core Ops, SparseCore 0:
  35.2 46.3 all-gather.1

commit v2 on v1

v2 whole, which is shorter than its diff:
```python
import functools

import jax
import jax.numpy as jnp
from jax import lax
from jax.experimental import pallas as pl
from jax.experimental.pallas import tpu as pltpu
from jax.sharding import PartitionSpec as P

HD = 128
BLK = 128
DROWS = 128
STEPS = 4
OWNERS = 4
HALVES = 2

LOWEST = -1e30
LOG2E = 1.4426950408889634
SCALE = LOG2E * HD ** (-0.5)


def source_rank(owner_of, rank_here, ranks):
    index = jnp.arange(ranks, dtype=jnp.int32)
    same = owner_of[None, :] == owner_of[:, None]
    earlier = index[None, :] < index[:, None]
    before = jnp.sum((same & earlier).astype(jnp.int32), axis=1)
    dest = owner_of * (ranks // OWNERS) + before
    return jnp.sum(jnp.where(dest == rank_here, index, 0))


def attend(order_ref, plan_ref, query_ref, dec_query_ref, limits_ref, pairs_refs, first_item, state):
    rows = query_ref.shape[0]
    heads = query_ref.shape[1] // HD
    lane = lax.broadcasted_iota(jnp.int32, (1, rows), 1)
    line = lax.broadcasted_iota(jnp.int32, (rows, HD), 0)

    def places(rank, index):
        low = order_ref[rank * 2] * BLK
        high = order_ref[rank * 2 + 1] * BLK - BLK
        return jnp.where(index < BLK, low, high) + index

    query_places = places(plan_ref[0], line)
    items = []
    for ref in pairs_refs:
        for start in range(0, ref.shape[0], 2 * rows):
            items.append((ref, start, places(plan_ref[1 + first_item + len(items)], lane)))
    for group in range(heads + 1):
        if group < heads:
            query = query_ref[:, group * HD : (group + 1) * HD]
            row_places = query_places
        else:
            query = dec_query_ref[...]
            row_places = limits_ref[...] - 1
        row_places = jnp.tile(row_places, (1, rows // HD))
        acc, total, top = state(group)
        for ref, start, key_places in items:
            key_rows = ref[start : start + rows, :]
            value_rows = ref[start + rows : start + 2 * rows, :]
            scores = lax.dot_general(
                query, key_rows, (((1,), (1,)), ((), ())), preferred_element_type=jnp.float32
            )
            scores = jnp.where(row_places >= key_places, scores, LOWEST)
            new_top = jnp.maximum(top, jnp.max(scores, axis=1, keepdims=True))
            weights = jnp.exp2(scores * SCALE - jnp.tile(new_top * SCALE, (1, rows // HD)))
            fade = jnp.exp2((top - new_top) * SCALE)
            wide = jnp.concatenate([value_rows, jnp.ones_like(value_rows)], axis=1)
            mixed = jnp.dot(
                weights.astype(jnp.bfloat16), wide, preferred_element_type=jnp.float32
            )
            acc = acc * fade + mixed[:, 0:HD]
            total = total * fade + mixed[:, HD : 2 * HD]
            top = new_top
        yield group, acc, total, top


def empty_state(rows):
    def state(group):
        zero = jnp.zeros((rows, HD), jnp.float32)
        return zero, zero, jnp.full((rows, HD), LOWEST, jnp.float32)

    return state


def held_state(state_ref):
    def state(group):
        return tuple(state_ref[group, :, part * HD : (part + 1) * HD] for part in range(3))

    return state


def first_kernel(order_ref, plan_ref, query_ref, dec_query_ref, limits_ref, pairs_ref, state_ref):
    state = empty_state(query_ref.shape[0])
    refs = (order_ref, plan_ref, query_ref, dec_query_ref, limits_ref, (pairs_ref,))
    for group, *parts in attend(*refs, 0, state):
        for part, value in enumerate(parts):
            state_ref[group, :, part * HD : (part + 1) * HD] = value


def next_kernel(
    first_item, order_ref, plan_ref, query_ref, dec_query_ref, limits_ref, right_ref, left_ref, held_ref, state_ref
):
    state = held_state(held_ref)
    refs = (order_ref, plan_ref, query_ref, dec_query_ref, limits_ref, (right_ref, left_ref))
    for group, *parts in attend(*refs, first_item, state):
        for part, value in enumerate(parts):
            state_ref[group, :, part * HD : (part + 1) * HD] = value


def last_kernel(
    first_item,
    places,
    order_ref,
    plan_ref,
    pick_ref,
    query_ref,
    dec_query_ref,
    limits_ref,
    pairs_ref,
    held_ref,
    *rest,
):
    sources = rest[:places]
    out_ref, owned_keys_ref, owned_values_ref, dec_out_ref, out_rows, dec_rows, out_sems, owned_sems, dec_sem = rest[
        places:
    ]
    rows = query_ref.shape[0]
    heads = query_ref.shape[1] // HD
    steps, share = dec_out_ref.shape[0], dec_out_ref.shape[1]

    def hand_over(source, offset):
        keys = source.at[pl.ds(offset, rows), :]
        values = source.at[pl.ds(offset + rows, rows), :]
        return (
            pltpu.make_async_copy(keys, owned_keys_ref, owned_sems.at[0]),
            pltpu.make_async_copy(values, owned_values_ref, owned_sems.at[1]),
        )

    for place, source in enumerate(sources):

        @pl.when(pick_ref[0] == place)
        def _(source=source):
            for copy in hand_over(source, pl.multiple_of(pick_ref[1], rows)):
                copy.start()

    copies = []
    refs = (order_ref, plan_ref, query_ref, dec_query_ref, limits_ref, (pairs_ref,))
    for group, acc, total, _ in attend(*refs, first_item, held_state(held_ref)):
        mixed = (acc / total).astype(jnp.bfloat16)
        if group < heads:
            across = pl.ds(group * HD, HD)
            out_rows[group] = mixed
            copies.append(pltpu.make_async_copy(out_rows.at[group], out_ref.at[:, across], out_sems.at[group]))
        else:
            for head in range(heads):
                piece = mixed[head * steps * share : (head + 1) * steps * share]
                dec_rows[:, :, head * HD : (head + 1) * HD] = piece.reshape(steps, share, HD)
            copies.append(pltpu.make_async_copy(dec_rows, dec_out_ref, dec_sem))
        copies[-1].start()
    for copy in copies:
        copy.wait()
    for copy in hand_over(sources[0], 0):
        copy.wait()


def per_device(queries, keys, values, block_order, owner_of, dec_queries, dec_pos):
    rows = queries.shape[0]
    heads = queries.shape[1] // HD
    groups = heads + 1
    ranks = lax.axis_size("ctx")
    rank_here = lax.axis_index("ctx")
    along = ranks // HALVES
    share = DROWS // ranks
    place_here = rank_here % along

    def shift(block, by):
        moves = []
        for rank in range(ranks):
            half, place = rank // along, rank % along
            moves.append((rank, half * along + (place + by) % along))
        return lax.ppermute(block, "ctx", moves)

    across = [[half * along + place for half in range(HALVES)] for place in range(along)]
    pair = jnp.concatenate([keys, values], axis=0)
    here = lax.all_gather(pair, "ctx", axis=0, axis_index_groups=across, tiled=True)
    rights, lefts = [here], [here]
    for step in range(1, along // 2):
        rights.append(shift(rights[-1], -1))
        lefts.append(shift(lefts[-1], 1))
    opposite = shift(rights[-1], -1)

    dec_mine = lax.dynamic_slice_in_dim(dec_queries, rank_here * share, share, 1)
    dec_query = jnp.transpose(dec_mine.reshape(STEPS * share, heads, HD), (1, 0, 2)).reshape(-1, HD)
    limits = lax.dynamic_slice_in_dim(dec_pos, rank_here * share, share, 1).reshape(-1)
    limits = jnp.broadcast_to(jnp.tile(limits, (heads,))[:, None], (rows, HD))

    distances = [0]
    for step in range(1, along // 2):
        distances += [step, -step]
    distances.append(along // 2)
    held_at = [(place_here + distance) % along for distance in distances]
    plan = [rank_here] + [half * along + place for place in held_at for half in range(HALVES)]
    plan = jnp.stack(plan).astype(jnp.int32)

    source = source_rank(owner_of, rank_here, ranks)
    found = jnp.stack(held_at) == source % along
    pick = jnp.stack([jnp.argmax(found).astype(jnp.int32), (source // along) * 2 * rows])

    smem = pl.BlockSpec(memory_space=pltpu.SMEM)
    vmem = pl.BlockSpec(memory_space=pltpu.VMEM)
    anywhere = pl.BlockSpec(memory_space=pl.ANY)
    state_shape = jax.ShapeDtypeStruct((groups, rows, 3 * HD), jnp.float32)
    fixed = (queries, dec_query, limits)

    def cost(items):
        return pl.CostEstimate(
            flops=8 * groups * rows * items * rows * HD,
            bytes_accessed=items * rows * HD * 4,
            transcendentals=groups * rows * items * rows,
        )

    params = pltpu.CompilerParams(vmem_limit_bytes=24 * 2**20)
    state = pl.pallas_call(
        first_kernel,
        in_specs=[smem] * 2 + [vmem] * 4,
        out_specs=vmem,
        out_shape=state_shape,
        compiler_params=params,
        cost_estimate=cost(HALVES),
        name="attend_here",
    )(block_order, plan, *fixed, here)
    for step in range(1, along // 2):
        state = pl.pallas_call(
            functools.partial(next_kernel, HALVES * (2 * step - 1)),
            in_specs=[smem] * 2 + [vmem] * 6,
            out_specs=vmem,
            out_shape=state_shape,
            compiler_params=params,
            cost_estimate=cost(2 * HALVES),
            name=f"attend_{step}",
        )(block_order, plan, *fixed, rights[step], lefts[step], state)
    sources = [here]
    for step in range(1, along // 2):
        sources += [rights[step], lefts[step]]
    sources.append(opposite)
    return pl.pallas_call(
        functools.partial(last_kernel, HALVES * (along - 1), len(sources)),
        in_specs=[smem] * 3 + [vmem] * 5 + [anywhere] * len(sources),
        out_specs=[anywhere] * 4,
        out_shape=[
            jax.ShapeDtypeStruct(queries.shape, queries.dtype),
            jax.ShapeDtypeStruct(keys.shape, keys.dtype),
            jax.ShapeDtypeStruct(values.shape, values.dtype),
            jax.ShapeDtypeStruct((STEPS, share, heads * HD), queries.dtype),
        ],
        scratch_shapes=[
            pltpu.VMEM((heads, rows, HD), jnp.bfloat16),
            pltpu.VMEM((STEPS, share, heads * HD), jnp.bfloat16),
            pltpu.SemaphoreType.DMA((heads,)),
            pltpu.SemaphoreType.DMA((2,)),
            pltpu.SemaphoreType.DMA(()),
        ],
        compiler_params=params,
        cost_estimate=cost(HALVES),
        name="attend_last",
    )(block_order, plan, pick, *fixed, opposite, state, *sources)


def solution(mesh):
    placed = (
        P(("req", "ctx"), "head"),
        P(("req", "ctx"), "head"),
        P(("req", "ctx"), "head"),
        P("req"),
        P("req"),
        P("req", None, "head"),
        P("req", None),
    )
    return jax.shard_map(
        per_device,
        mesh=mesh,
        in_specs=placed,
        out_specs=(
            P(("req", "ctx"), "head"),
            P(("req", "ctx"), "head"),
            P(("req", "ctx"), "head"),
            P("req", "ctx", "head"),
        ),
        check_vma=False,
    )
```

time: 105 us -> 75.6 us (0.72)
  the two profiles are of different devices: /device:TPU:6 before, /device:TPU:66 now
where the time goes in v2:
time: 75.6 us; the launch traced here: 75.1 us
  starting transfers between devices  26.7 us (35%)
  Pallas kernels  22.3 us (29%)
  blocking collectives  15.2 us (20%)
  other arithmetic  4.68 us (6%)
  between operations  3.3 us (4%)
  local copies, waits for them, and re-layouts  2.94 us (4%)
    ppermute x7, starting transfers between devices, shift(): return lax.ppermute(block, 'ctx', moves)  26.7 us
    pallas_call x3, Pallas kernels, per_device(): pl.pallas_call(functools.partial(next_kernel, HALVES * (2 * step - 1)), i...  15.6 us
    all_gather x1, blocking collectives, per_device(): lax.all_gather(pair, 'ctx', axis=0, axis_index_groups=across, tiled=True)  15.2 us
    pallas_call x1, Pallas kernels, per_device(): pl.pallas_call(functools.partial(last_kernel, HALVES * (along - 1), len(s...  3.91 us
    pallas_call x1, Pallas kernels, per_device(): pl.pallas_call(first_kernel, in_specs=[smem] * 2 + [vmem] * 4, out_specs=...  2.77 us
    unnamed x8, local copies, waits for them, and re-layouts  1.73 us
  transfers between devices with their start and end apart: 7, of which 0 were waited for; matrix products, arithmetic and copies ran while one was open for 7% of the time, Pallas kernels for 24%

profile of v2, /device:TPU:66, one launch (start us, length us, event | category | flops | bytes accessed | tf_op | source)
XLA Modules:
  0.0 75.1 jit_solution(582465139164510854)
XLA Ops:
  0.6 0.0 copy-start
  0.6 1.0 %pad_maximum_fusion = bf16[512,128]{1,0:T(8,128)(2,1)S(1)} fusion(bf16[256,128]{1,0:T(8,128)(2,1)} %param.9, bf16[256,128]{1,0:T(8,128)(2,1)} %param.8), kind=kLoop, calls=%fused_computation | loop fusion | flops 262144 | bytes 262144 | tf_op jit(solution)/shard_map/concatenate | solution.py:183
  1.6 15.2 %all_gather.3.pairs_ref.rest_0_ = bf16[1024,128]{1,0:T(8,128)(2,1)S(1)} all-gather(bf16[512,128]{1,0:T(8,128)(2,1)S(1)} %pad_maximum_fusion), channel_id=1, replica_groups={{0,256},{32,288},{64,320},{96,352},{128,384},{160,416},{192,448},{224,4..., dimensions={0}, use_global_device_ids=true | all-gather | bytes 393216 | tf_op jit(solution)/shard_map/all_gather | solution.py:184
  16.8 5.4 %collective-permute-start = (bf16[1024,128]{1,0:T(8,128)(2,1)S(1)}, bf16[1024,128]{1,0:T(8,128)(2,1)S(1)}, u32[]{:S(2)}, u32[]{:S(2)}) collective-permute-start(bf16[1024,128]{1,0:T(8,128)(2,1)S(1)} %all_gather.3.pairs_ref.rest_0_), channel_id=1, source_target_pairs={{0,224},{32,0},{64,32},{96,64},{128,96},{160,128},{192,160},{224,1... | collective-permute-start | bytes 786440 | tf_op jit(solution)/shard_map/ppermute | solution.py:180
  22.2 1.9 %collective-permute-start.4 = (bf16[1024,128]{1,0:T(8,128)(2,1)S(1)}, bf16[1024,128]{1,0:T(8,128)(2,1)S(1)}, u32[]{:S(2)}, u32[]{:S(2)}) collective-permute-start(bf16[1024,128]{1,0:T(8,128)(2,1)S(1)} %all_gather.3.pairs_ref.rest_0_), channel_id=1, source_target_pairs={{0,32},{32,64},{64,96},{96,128},{128,160},{160,192},{192,224},{224... | collective-permute-start | bytes 786440 | tf_op jit(solution)/shard_map/ppermute | solution.py:180
  24.1 0.9 %convert_reduce_fusion = s32[16]{0:T(128)S(1)} fusion(s32[16]{0:T(128)} %param.11), kind=kLoop, calls=%fused_computation.2 | loop fusion | flops 1264 | bytes 128 | tf_op jit(solution)/shard_map/reduce_sum | solution.py:26
  25.1 1.3 %fusion.1 = s32[]{:T(128)} fusion(s32[16]{0:T(128)S(1)} %convert_reduce_fusion, s32[16]{0:T(128)} %param.11, s32[]{:T(128)} %axis_index.15), kind=kLoop, calls=%fused_computation.7 | loop fusion | flops 79 | bytes 136 | tf_op jit(solution)/shard_map/reduce_sum | solution.py:28
  28.1 0.1 stack.92
  28.2 0.7 compare_reduce_fusion
  28.9 0.0 collective-permute-done.right_ref.rest_1_
  28.9 5.1 %collective-permute-start.1 = (bf16[1024,128]{1,0:T(8,128)(2,1)S(1)}, bf16[1024,128]{1,0:T(8,128)(2,1)S(1)}, u32[]{:S(2)}, u32[]{:S(2)}) collective-permute-start(bf16[1024,128]{1,0:T(8,128)(2,1)S(1)} %collective-permute-done.right_ref.rest_1_), channel_id=1, source_target_pairs={{0,224},{32,0},{64,32},{96,64},{128,96},{160,128},{192,160},{224,1... | collective-permute-start | bytes 786440 | tf_op jit(solution)/shard_map/ppermute | solution.py:180
  34.1 0.0 copy-done
  34.1 0.0 collective-permute-done.4.left_ref.rest_2_
  34.1 1.9 %collective-permute-start.5 = (bf16[1024,128]{1,0:T(8,128)(2,1)S(1)}, bf16[1024,128]{1,0:T(8,128)(2,1)S(1)}, u32[]{:S(2)}, u32[]{:S(2)}) collective-permute-start(bf16[1024,128]{1,0:T(8,128)(2,1)S(1)} %collective-permute-done.4.left_ref.rest_2_), channel_id=1, source_target_pairs={{0,32},{32,64},{64,96},{96,128},{128,160},{160,192},{192,224},{224... | collective-permute-start | bytes 786440 | tf_op jit(solution)/shard_map/ppermute | solution.py:180
  36.0 0.8 %constant_dynamic-slice_fusion = s32[4,8]{1,0:T(4,128)S(1)} fusion(s32[4,128]{1,0:T(4,128)} %param.13, s32[]{:T(128)S(6)} %select_n.71), kind=kLoop, calls=%fused_computation.9 | loop fusion | bytes 260 | tf_op jit(solution)/shard_map/dynamic_slice | solution.py:193
  37.4 0.1 tile.7
  37.5 0.1 broadcast_in_dim.16
  37.6 0.1 stack.91.plan_ref
  37.7 0.1 broadcast_in_dim.17.limits_ref
  37.8 0.0 copy-start.1
  37.8 1.0 %copy-done.1 = bf16[256,1024]{1,0:T(8,128)(2,1)S(1)} copy-done((bf16[256,1024]{1,0:T(8,128)(2,1)S(1)}, bf16[256,1024]{1,0:T(8,128)(2,1)}, u32[]{:S(2)}) %copy-start.1) | copy-done | bytes 524312
  38.8 0.0 copy-start.2
  38.8 0.7 copy-done.2
  39.5 2.8 %attend_here.1.held_ref = f32[9,256,384]{2,1,0:T(8,128)S(1)} custom-call(s32[32]{0:T(128)S(1)} %copy-done.2, s32[17]{0:T(128)S(1)} %stack.91.plan_ref, bf16[256,1024]{1,0:T(8,128)(2,1)S(1)} %copy-done.1, bf16[256,128]{1,0:T(8,128)(2,1)S(1)} %bitcast.26, s32[256,128]{1,0:T(8,128)S(1)} %broadcast_in_dim.17.limits_ref, ...), custom_call_target="tpu_custom_call" | custom-call | flops 1207959552 | bytes 262144 | tf_op jit(solution)/shard_map/attend_here/pallas_call | solution.py:222
  42.2 0.0 collective-permute-done.1.right_ref.rest_3_
  42.3 5.1 %collective-permute-start.2 = (bf16[1024,128]{1,0:T(8,128)(2,1)S(1)}, bf16[1024,128]{1,0:T(8,128)(2,1)S(1)}, u32[]{:S(2)}, u32[]{:S(2)}) collective-permute-start(bf16[1024,128]{1,0:T(8,128)(2,1)S(1)} %collective-permute-done.1.right_ref.rest_3_), channel_id=1, source_target_pairs={{0,224},{32,0},{64,32},{96,64},{128,96},{160,128},{192,160},{224,1... | collective-permute-start | bytes 786440 | tf_op jit(solution)/shard_map/ppermute | solution.py:180
  47.4 0.8 %pad_add_fusion.pick_ref = s32[2]{0:T(128)S(1)} fusion(s32[1]{0:T(128)} %bitcast.18, s32[1]{0:T(128)} %bitcast.17), kind=kLoop, calls=%fused_computation.8 | loop fusion | flops 2 | bytes 16 | tf_op jit(solution)/shard_map/stack | solution.py:206
  48.2 0.0 collective-permute-done.5.left_ref.rest_4_
  48.2 1.9 %collective-permute-start.6 = (bf16[1024,128]{1,0:T(8,128)(2,1)S(1)}, bf16[1024,128]{1,0:T(8,128)(2,1)S(1)}, u32[]{:S(2)}, u32[]{:S(2)}) collective-permute-start(bf16[1024,128]{1,0:T(8,128)(2,1)S(1)} %collective-permute-done.5.left_ref.rest_4_), channel_id=1, source_target_pairs={{0,32},{32,64},{64,96},{96,128},{128,160},{160,192},{192,224},{224... | collective-permute-start | bytes 786440 | tf_op jit(solution)/shard_map/ppermute | solution.py:180
  50.1 5.2 %attend_1.1.held_ref = f32[9,256,384]{2,1,0:T(8,128)S(1)} custom-call(s32[32]{0:T(128)S(1)} %copy-done.2, s32[17]{0:T(128)S(1)} %stack.91.plan_ref, bf16[256,1024]{1,0:T(8,128)(2,1)S(1)} %copy-done.1, bf16[256,128]{1,0:T(8,128)(2,1)S(1)} %bitcast.27, s32[256,128]{1,0:T(8,128)S(1)} %broadcast_in_dim.17.limits_ref, ...), custom_call_target="tpu_custom_call" | custom-call | flops 2415919104 | bytes 524288 | tf_op jit(solution)/shard_map/attend_1/pallas_call | solution.py:232
  55.2 0.0 collective-permute-done.2.right_ref.rest_5_
  55.3 5.3 %collective-permute-start.3 = (bf16[1024,128]{1,0:T(8,128)(2,1)S(1)}, bf16[1024,128]{1,0:T(8,128)(2,1)S(1)}, u32[]{:S(2)}, u32[]{:S(2)}) collective-permute-start(bf16[1024,128]{1,0:T(8,128)(2,1)S(1)} %collective-permute-done.2.right_ref.rest_5_), channel_id=1, source_target_pairs={{0,224},{32,0},{64,32},{96,64},{128,96},{160,128},{192,160},{224,1... | collective-permute-start | bytes 786440 | tf_op jit(solution)/shard_map/ppermute | solution.py:180
  60.6 5.2 %attend_2.1.held_ref = f32[9,256,384]{2,1,0:T(8,128)S(1)} custom-call(s32[32]{0:T(128)S(1)} %copy-done.2, s32[17]{0:T(128)S(1)} %stack.91.plan_ref, bf16[256,1024]{1,0:T(8,128)(2,1)S(1)} %copy-done.1, bf16[256,128]{1,0:T(8,128)(2,1)S(1)} %bitcast.28, s32[256,128]{1,0:T(8,128)S(1)} %broadcast_in_dim.17.limits_ref, ...), custom_call_target="tpu_custom_call" | custom-call | flops 2415919104 | bytes 524288 | tf_op jit(solution)/shard_map/attend_2/pallas_call | solution.py:232
  65.7 0.0 collective-permute-done.6.left_ref.rest_6_
  65.7 5.3 %attend_3.1.held_ref = f32[9,256,384]{2,1,0:T(8,128)S(1)} custom-call(s32[32]{0:T(128)S(1)} %copy-done.2, s32[17]{0:T(128)S(1)} %stack.91.plan_ref, bf16[256,1024]{1,0:T(8,128)(2,1)S(1)} %copy-done.1, bf16[256,128]{1,0:T(8,128)(2,1)S(1)} %bitcast.29, s32[256,128]{1,0:T(8,128)S(1)} %broadcast_in_dim.17.limits_ref, ...), custom_call_target="tpu_custom_call" | custom-call | flops 2415919104 | bytes 524288 | tf_op jit(solution)/shard_map/attend_3/pallas_call | solution.py:232
  71.1 0.0 collective-permute-done.3.pairs_ref.rest_7_
  71.1 3.9 %attend_last.1 = (bf16[256,1024]{1,0:T(8,128)(2,1)}, bf16[256,128]{1,0:T(8,128)(2,1)}, bf16[256,128]{1,0:T(8,128)(2,1)}, bf16[4,8,1024]{2,1,0:T(8,128)(2,1)}) custom-call(s32[32]{0:T(128)S(1)} %copy-done.2, s32[17]{0:T(128)S(1)} %stack.91.plan_ref, s32[2]{0:T(128)S(1)} %pad_add_fusion.pick_ref, bf16[256,1024]{1,0:T(8,128)(2,1)S(1)} %copy-done.1, ...), custom_call_target="tpu_custom_call" | custom-call | flops 1207959552 | bytes 262144 | tf_op jit(solution)/shard_map/attend_last/pallas_call | solution.py:245
  (4 shorter events, 0.0 us)
Async XLA Ops:
  0.6 33.4 %copy-start = (bf16[4,128,1024]{2,1,0:T(8,128)(2,1)S(1)}, bf16[4,128,1024]{2,1,0:T(8,128)(2,1)}, u32[]{:S(2)}) copy-start(bf16[4,128,1024]{2,1,0:T(8,128)(2,1)} %param.12) | copy-start | bytes 3145732
  16.8 12.1 %collective-permute-start = (bf16[1024,128]{1,0:T(8,128)(2,1)S(1)}, bf16[1024,128]{1,0:T(8,128)(2,1)S(1)}, u32[]{:S(2)}, u32[]{:S(2)}) collective-permute-start(bf16[1024,128]{1,0:T(8,128)(2,1)S(1)} %all_gather.3.pairs_ref.rest_0_), channel_id=1, source_target_pairs={{0,224},{32,0},{64,32},{96,64},{128,96},{160,128},{192,160},{224,1... | collective-permute-start | bytes 786440 | tf_op jit(solution)/shard_map/ppermute | solution.py:180
  22.2 11.9 %collective-permute-start.4 = (bf16[1024,128]{1,0:T(8,128)(2,1)S(1)}, bf16[1024,128]{1,0:T(8,128)(2,1)S(1)}, u32[]{:S(2)}, u32[]{:S(2)}) collective-permute-start(bf16[1024,128]{1,0:T(8,128)(2,1)S(1)} %all_gather.3.pairs_ref.rest_0_), channel_id=1, source_target_pairs={{0,32},{32,64},{64,96},{96,128},{128,160},{160,192},{192,224},{224... | collective-permute-start | bytes 786440 | tf_op jit(solution)/shard_map/ppermute | solution.py:180
  28.9 13.3 %collective-permute-start.1 = (bf16[1024,128]{1,0:T(8,128)(2,1)S(1)}, bf16[1024,128]{1,0:T(8,128)(2,1)S(1)}, u32[]{:S(2)}, u32[]{:S(2)}) collective-permute-start(bf16[1024,128]{1,0:T(8,128)(2,1)S(1)} %collective-permute-done.right_ref.rest_1_), channel_id=1, source_target_pairs={{0,224},{32,0},{64,32},{96,64},{128,96},{160,128},{192,160},{224,1... | collective-permute-start | bytes 786440 | tf_op jit(solution)/shard_map/ppermute | solution.py:180
  34.1 14.1 %collective-permute-start.5 = (bf16[1024,128]{1,0:T(8,128)(2,1)S(1)}, bf16[1024,128]{1,0:T(8,128)(2,1)S(1)}, u32[]{:S(2)}, u32[]{:S(2)}) collective-permute-start(bf16[1024,128]{1,0:T(8,128)(2,1)S(1)} %collective-permute-done.4.left_ref.rest_2_), channel_id=1, source_target_pairs={{0,32},{32,64},{64,96},{96,128},{128,160},{160,192},{192,224},{224... | collective-permute-start | bytes 786440 | tf_op jit(solution)/shard_map/ppermute | solution.py:180
  37.8 1.0 %copy-start.1 = (bf16[256,1024]{1,0:T(8,128)(2,1)S(1)}, bf16[256,1024]{1,0:T(8,128)(2,1)}, u32[]{:S(2)}) copy-start(bf16[256,1024]{1,0:T(8,128)(2,1)} %query_ref.9) | copy-start | bytes 1572868
  38.8 0.7 copy-start.2
  42.3 13.0 %collective-permute-start.2 = (bf16[1024,128]{1,0:T(8,128)(2,1)S(1)}, bf16[1024,128]{1,0:T(8,128)(2,1)S(1)}, u32[]{:S(2)}, u32[]{:S(2)}) collective-permute-start(bf16[1024,128]{1,0:T(8,128)(2,1)S(1)} %collective-permute-done.1.right_ref.rest_3_), channel_id=1, source_target_pairs={{0,224},{32,0},{64,32},{96,64},{128,96},{160,128},{192,160},{224,1... | collective-permute-start | bytes 786440 | tf_op jit(solution)/shard_map/ppermute | solution.py:180
  48.2 17.6 %collective-permute-start.6 = (bf16[1024,128]{1,0:T(8,128)(2,1)S(1)}, bf16[1024,128]{1,0:T(8,128)(2,1)S(1)}, u32[]{:S(2)}, u32[]{:S(2)}) collective-permute-start(bf16[1024,128]{1,0:T(8,128)(2,1)S(1)} %collective-permute-done.5.left_ref.rest_4_), channel_id=1, source_target_pairs={{0,32},{32,64},{64,96},{96,128},{128,160},{160,192},{192,224},{224... | collective-permute-start | bytes 786440 | tf_op jit(solution)/shard_map/ppermute | solution.py:180
  55.3 15.8 %collective-permute-start.3 = (bf16[1024,128]{1,0:T(8,128)(2,1)S(1)}, bf16[1024,128]{1,0:T(8,128)(2,1)S(1)}, u32[]{:S(2)}, u32[]{:S(2)}) collective-permute-start(bf16[1024,128]{1,0:T(8,128)(2,1)S(1)} %collective-permute-done.2.right_ref.rest_5_), channel_id=1, source_target_pairs={{0,224},{32,0},{64,32},{96,64},{128,96},{160,128},{192,160},{224,1... | collective-permute-start | bytes 786440 | tf_op jit(solution)/shard_map/ppermute | solution.py:180

commit v3 on v2

v3 whole, which is shorter than its diff:
```python
import functools

import jax
import jax.numpy as jnp
from jax import lax
from jax.experimental import pallas as pl
from jax.experimental.pallas import tpu as pltpu
from jax.sharding import PartitionSpec as P

HD = 128
BLK = 128
DROWS = 128
STEPS = 4
OWNERS = 4
HALVES = 2
TILE = 16
TOGETHER = 2

LOWEST = -1e30
LOG2E = 1.4426950408889634
SCALE = LOG2E * HD ** (-0.5)
REACH = 64.0


def largest_norm(rows):
    lengths = jnp.sum(rows * rows, axis=1, keepdims=True)
    return jnp.max(lengths, axis=0, keepdims=True)


def attend(refs, pairs_refs, places_of, along, calm, was_calm, sums_ref, tops_ref, emit, settle=lambda: None):
    here_ref, order_ref, query_ref, dec_query_ref, limits_ref = refs
    rows, heads = query_ref.shape[0], query_ref.shape[1] // HD
    groups = heads + 1
    here = here_ref[0]
    lane = lax.broadcasted_iota(jnp.int32, (1, rows), 1)
    line = lax.broadcasted_iota(jnp.int32, (rows, HD), 0)

    def places(rank, index):
        low = order_ref[rank * 2] * BLK
        high = order_ref[rank * 2 + 1] * BLK - BLK
        return jnp.where(index < BLK, low, high) + index

    query_places = places(here, line)
    dec_places = jnp.tile(limits_ref[...] - 1, (heads, 1))
    blocks = [(ref, start) for ref in pairs_refs for start in range(0, ref.shape[0], 2 * rows)]
    items = []
    for (ref, start), (distance, other) in zip(blocks, places_of):
        half = here // along
        half = 1 - half if other else half
        rank = half * along + lax.rem(here + distance + along, along)
        items.append((ref, start, places(rank, lane)))

    def item_rows(part):
        keys = [ref[start : start + rows, :] for ref, start, _ in part]
        values = [ref[start + rows : start + 2 * rows, :] for ref, start, _ in part]
        wide = [jnp.concatenate([value, jnp.ones_like(value)], axis=1) for value in values]
        return jnp.concatenate(keys, axis=0), jnp.concatenate(wide, axis=0)

    def masked(query, keys, part, row_places):
        scores = lax.dot_general(query, keys, (((1,), (1,)), ((), ())), preferred_element_type=jnp.float32)
        key_places = jnp.concatenate([key_places for _, _, key_places in part], axis=1)
        visible = jnp.tile(row_places, (1, key_places.shape[1] // HD)) >= key_places
        return jnp.where(visible, scores * SCALE, LOWEST)

    parts = [items[first : first + TOGETHER] for first in range(0, len(items), TOGETHER)]

    def start_sums(group):
        return jnp.zeros((rows, 2 * HD), jnp.float32) if sums_ref is None else sums_ref[group]

    for group in range(groups):
        row_places = query_places if group < heads else dec_places
        query = query_ref[:, group * HD : (group + 1) * HD] if group < heads else dec_query_ref[...]
        sums = start_sums(group)
        for part in parts:
            keys, wide = item_rows(part)
            weights = jnp.exp2(masked(query, keys, part, row_places))
            sums += jnp.dot(weights.astype(jnp.bfloat16), wide, preferred_element_type=jnp.float32)
        emit(group, sums, None)

    @pl.when(jnp.logical_not(calm))
    def _():
        settle()

        def visit(group, _):
            row_places = jnp.where(group < heads, query_places, dec_places)
            across = pl.ds(pl.multiple_of(jnp.minimum(group, heads - 1) * HD, HD), HD)
            query = jnp.where(group < heads, query_ref[:, across], dec_query_ref[...])
            sums = start_sums(group)
            top = jnp.where(sums[:, HD:] > 0.0, 0.0, LOWEST)
            if tops_ref is not None:
                top = jnp.where(was_calm, top, tops_ref[group])
            for part in parts:
                keys, wide = item_rows(part)
                scores = masked(query, keys, part, row_places)
                new_top = jnp.maximum(top, jnp.max(scores, axis=1, keepdims=True))
                weights = jnp.exp2(scores - jnp.tile(new_top, (1, scores.shape[1] // HD)))
                fade = jnp.tile(jnp.exp2(top - new_top), (1, 2))
                sums = sums * fade + jnp.dot(
                    weights.astype(jnp.bfloat16), wide, preferred_element_type=jnp.float32
                )
                top = new_top
            emit(group, sums, top)
            return 0

        lax.fori_loop(0, groups, visit, 0)


def reach_of(query_norm, key_norm):
    return jnp.max(query_norm * key_norm)


def key_norms(pairs_refs, rows):
    norm = None
    for ref in pairs_refs:
        for start in range(0, ref.shape[0], 2 * rows):
            found = largest_norm(ref[start : start + rows, :].astype(jnp.float32))
            norm = found if norm is None else jnp.maximum(norm, found)
    return norm


def first_kernel(
    along, here_ref, order_ref, limit_ref, query_ref, dec_ref, pairs_ref, dec_query_ref, limits_ref, norms_ref, sums_ref, tops_ref, dec_rows
):
    rows, heads = query_ref.shape[0], query_ref.shape[1] // HD
    steps, share = dec_ref.shape[0], limits_ref.shape[0] // dec_ref.shape[0]
    first = here_ref[0] * share
    base = pl.multiple_of(first // TILE * TILE, TILE)
    for head in range(heads):
        for step in range(steps):
            block = dec_ref[step, pl.ds(base, TILE), head * HD : (head + 1) * HD].astype(jnp.float32)
            mine = block[0:share]
            for other in range(share, TILE, share):
                mine = jnp.where(first - base == other, block[other : other + share], mine)
            dec_rows[(head * steps + step) * share : (head * steps + step + 1) * share, :] = mine
    for step in range(steps):
        for row in range(share):
            limits_ref[step * share + row : step * share + row + 1, :] = jnp.full(
                (1, HD), limit_ref[step, first + row], jnp.int32
            )
    dec_query_ref[...] = dec_rows[...].astype(jnp.bfloat16)
    query_norm = largest_norm(dec_rows[...])
    for head in range(heads):
        query = query_ref[:, head * HD : (head + 1) * HD].astype(jnp.float32)
        query_norm = jnp.maximum(query_norm, largest_norm(query))
    query_norm = query_norm * (SCALE * SCALE)
    key_norm = key_norms((pairs_ref,), rows)
    norms_ref[0] = jnp.broadcast_to(query_norm, norms_ref.shape[1:])
    norms_ref[1] = jnp.broadcast_to(key_norm, norms_ref.shape[1:])
    calm = reach_of(query_norm, key_norm) <= REACH * REACH

    def emit(group, sums, top):
        sums_ref[group] = sums
        if top is not None:
            tops_ref[group] = top

    refs = (here_ref, order_ref, query_ref, dec_query_ref, limits_ref)
    attend(refs, (pairs_ref,), ((0, False),), along, calm, True, None, None, emit)


def norms_so_far(norms_ref, pairs_refs, rows):
    query_norm, before = norms_ref[0], norms_ref[1]
    now = jnp.maximum(before, key_norms(pairs_refs, rows))
    bound = REACH * REACH
    return now, reach_of(query_norm, now) <= bound, reach_of(query_norm, before) <= bound


def next_kernel(along, places_of, blocks, here_ref, order_ref, query_ref, dec_query_ref, limits_ref, norms_in, sums_in, tops_in, *rest):
    pairs_refs = rest[:blocks]
    norms_ref, sums_ref, tops_ref = rest[blocks:]
    now, calm, was_calm = norms_so_far(norms_in, pairs_refs, query_ref.shape[0])
    norms_ref[0] = norms_in[0]
    norms_ref[1] = now

    def emit(group, sums, top):
        sums_ref[group] = sums
        if top is not None:
            tops_ref[group] = top

    refs = (here_ref, order_ref, query_ref, dec_query_ref, limits_ref)
    attend(refs, pairs_refs, places_of, along, calm, was_calm, sums_in, tops_in, emit)


def last_kernel(along, places_of, taken, arrivals, here_ref, order_ref, owner_ref, query_ref, dec_query_ref, limits_ref, norms_in, sums_in, tops_in, *rest):
    pairs_refs, rest = rest[:taken], rest[taken:]
    places = len(arrivals)
    sources = rest[:places]
    (out_ref, owned_keys_ref, owned_values_ref, dec_out_ref, out_rows, dec_rows, out_sems, owned_sems, dec_sem) = rest[places:]
    rows, heads = query_ref.shape[0], query_ref.shape[1] // HD
    steps, share = dec_out_ref.shape[0], dec_out_ref.shape[1]
    here = here_ref[0]

    ranks = owner_ref.shape[0]
    slots = ranks // OWNERS
    owner, turn = here // slots, here % slots
    source, seen = jnp.int32(0), jnp.int32(0)
    for rank in range(ranks):
        match = owner_ref[rank] == owner
        source = jnp.where(jnp.logical_and(match, seen == turn), rank, source)
        seen = seen + match.astype(jnp.int32)
    offset = pl.multiple_of(jnp.where(source // along == here // along, 0, 2 * rows), 2 * rows)
    apart = lax.rem(source - here + 2 * along, along)

    def hand_over(block, start):
        return (
            pltpu.make_async_copy(block.at[pl.ds(start, rows), :], owned_keys_ref, owned_sems.at[0]),
            pltpu.make_async_copy(block.at[pl.ds(start + rows, rows), :], owned_values_ref, owned_sems.at[1]),
        )

    for block, distance in zip(sources, arrivals):

        @pl.when(apart == distance % along)
        def _(block=block):
            for copy in hand_over(block, offset):
                copy.start()

    def emit_head(group, mixed):
        out_rows[group] = mixed
        out_copy(group).start()

    def emit_decode(mixed):
        for head in range(heads):
            piece = mixed[head * steps * share : (head + 1) * steps * share]
            dec_rows[:, :, head * HD : (head + 1) * HD] = piece.reshape(steps, share, HD)
        dec_copy.start()

    def out_copy(group):
        across = pl.ds(pl.multiple_of(group * HD, HD), HD)
        return pltpu.make_async_copy(out_rows.at[group], out_ref.at[:, across], out_sems.at[group])

    dec_copy = pltpu.make_async_copy(dec_rows, dec_out_ref, dec_sem)

    def emit(group, sums, top):
        mixed = (sums[:, 0:HD] / sums[:, HD:]).astype(jnp.bfloat16)
        if top is None:
            emit_head(group, mixed) if group < heads else emit_decode(mixed)
        else:
            pl.when(group < heads)(lambda: emit_head(group, mixed))
            pl.when(group == heads)(lambda: emit_decode(mixed))

    def settle():
        for group in range(heads):
            out_copy(group).wait()
        dec_copy.wait()

    _, calm, was_calm = norms_so_far(norms_in, pairs_refs, rows)
    refs = (here_ref, order_ref, query_ref, dec_query_ref, limits_ref)
    attend(refs, pairs_refs, places_of, along, calm, was_calm, sums_in, tops_in, emit, settle)
    settle()
    for copy in hand_over(sources[0], 0):
        copy.wait()


def pack_kernel(keys_ref, values_ref, pair_ref, sems):
    rows = keys_ref.shape[0]
    copies = (
        pltpu.make_async_copy(keys_ref, pair_ref.at[0:rows], sems.at[0]),
        pltpu.make_async_copy(values_ref, pair_ref.at[rows : 2 * rows], sems.at[1]),
    )
    for copy in copies:
        copy.start()
    for copy in copies:
        copy.wait()


def per_device(queries, keys, values, block_order, owner_of, dec_queries, dec_pos):
    rows = queries.shape[0]
    heads = queries.shape[1] // HD
    groups = heads + 1
    ranks = lax.axis_size("ctx")
    here = lax.axis_index("ctx").astype(jnp.int32).reshape(1)
    along = ranks // HALVES
    share = DROWS // ranks

    def shift(block, by):
        moves = []
        for rank in range(ranks):
            half, place = rank // along, rank % along
            moves.append((rank, half * along + (place + by) % along))
        return lax.ppermute(block, "ctx", moves)

    swap = [(rank, (rank + along) % ranks) for rank in range(ranks)]
    own = pl.pallas_call(
        pack_kernel,
        in_specs=[pl.BlockSpec(memory_space=pl.ANY)] * 2,
        out_specs=pl.BlockSpec(memory_space=pltpu.VMEM),
        out_shape=jax.ShapeDtypeStruct((2 * rows, HD), keys.dtype),
        scratch_shapes=[pltpu.SemaphoreType.DMA((2,))],
        name="pack",
    )(keys, values)
    other = lax.ppermute(own, "ctx", swap)
    local = jnp.concatenate([own, other], axis=0)
    rights, lefts = [local], [local]
    for step in range(1, along // 2):
        rights.append(shift(rights[-1], -1))
        lefts.append(shift(lefts[-1], 1))
    rounds = [{step: rights[step], -step: lefts[step]} for step in range(1, along // 2)]
    last = {along // 2: shift(rights[-1], -1)}

    smem = pl.BlockSpec(memory_space=pltpu.SMEM)
    vmem = pl.BlockSpec(memory_space=pltpu.VMEM)
    anywhere = pl.BlockSpec(memory_space=pl.ANY)
    shape = jax.ShapeDtypeStruct
    carried = [
        shape((2, 8, HD), jnp.float32),
        shape((groups, rows, 2 * HD), jnp.float32),
        shape((groups, rows, HD), jnp.float32),
    ]

    def cost(items):
        return pl.CostEstimate(
            flops=4 * 8 * groups * rows * items * rows * HD,
            bytes_accessed=items * rows * HD * 4,
            transcendentals=groups * rows * items * rows,
        )

    params = pltpu.CompilerParams(vmem_limit_bytes=24 * 2**20)
    dec_query, limits, *state = pl.pallas_call(
        functools.partial(first_kernel, along),
        in_specs=[smem] * 3 + [vmem] * 3,
        out_specs=[vmem] * 5,
        out_shape=[shape((rows, HD), jnp.bfloat16), shape((STEPS * share, HD), jnp.int32)] + carried,
        scratch_shapes=[pltpu.VMEM((rows, HD), jnp.float32)],
        compiler_params=params,
        cost_estimate=cost(1),
        name="attend_own",
    )(here, block_order, dec_pos, queries, dec_queries, own)
    fixed = (queries, dec_query, limits)

    def attend_more(state, blocks, places_of, name):
        return pl.pallas_call(
            functools.partial(next_kernel, along, places_of, len(blocks)),
            in_specs=[smem] * 2 + [vmem] * (6 + len(blocks)),
            out_specs=[vmem] * 3,
            out_shape=carried,
            compiler_params=params,
            cost_estimate=cost(max(len(places_of), 2 * HALVES)),
            name=name,
        )(here, block_order, *fixed, *state, *blocks)

    state = attend_more(state, [other], ((0, True),), "attend_other")
    def halves_of(blocks):
        return tuple((distance, other) for distance in blocks for other in (False, True))

    for number, blocks in enumerate(rounds):
        state = attend_more(state, list(blocks.values()), halves_of(blocks), f"attend_{number}")
    sources = {0: local}
    for blocks in rounds + [last]:
        sources.update(blocks)
    return pl.pallas_call(
        functools.partial(last_kernel, along, halves_of(last), len(last), tuple(sources)),
        in_specs=[smem] * 3 + [vmem] * (6 + len(last)) + [anywhere] * len(sources),
        out_specs=[anywhere] * 4,
        out_shape=[
            shape(queries.shape, queries.dtype),
            shape(keys.shape, keys.dtype),
            shape(values.shape, values.dtype),
            shape((STEPS, share, heads * HD), queries.dtype),
        ],
        scratch_shapes=[
            pltpu.VMEM((heads, rows, HD), jnp.bfloat16),
            pltpu.VMEM((STEPS, share, heads * HD), jnp.bfloat16),
            pltpu.SemaphoreType.DMA((heads,)),
            pltpu.SemaphoreType.DMA((2,)),
            pltpu.SemaphoreType.DMA(()),
        ],
        compiler_params=params,
        cost_estimate=cost(HALVES),
        name="attend_last",
    )(here, block_order, owner_of, *fixed, *state, *last.values(), *sources.values())


def solution(mesh):
    placed = (
        P(("req", "ctx"), "head"),
        P(("req", "ctx"), "head"),
        P(("req", "ctx"), "head"),
        P("req"),
        P("req"),
        P("req", None, "head"),
        P("req", None),
    )
    return jax.shard_map(
        per_device,
        mesh=mesh,
        in_specs=placed,
        out_specs=(
            P(("req", "ctx"), "head"),
            P(("req", "ctx"), "head"),
            P(("req", "ctx"), "head"),
            P("req", "ctx", "head"),
        ),
        check_vma=False,
    )
```

time: 75.6 us -> 94.2 us (1.25)
  the two profiles are of different devices: /device:TPU:66 before, /device:TPU:6 now
where the time goes in v3:
time: 94.2 us; the launch traced here: 93.7 us
  Pallas kernels  50.5 us (54%)
  starting transfers between devices  37.6 us (40%)
  local copies, waits for them, and re-layouts  4.52 us (5%)
  between operations  1.02 us (1%)
    pallas_call x4, Pallas kernels, attend_more(): pl.pallas_call(functools.partial(next_kernel, along, places_of, len(block...  34.8 us
    ppermute x7, starting transfers between devices, shift(): return lax.ppermute(block, 'ctx', moves)  26.7 us
    ppermute x1, starting transfers between devices, per_device(): other = lax.ppermute(own, 'ctx', swap)  10.9 us
    pallas_call x1, Pallas kernels, per_device(): pl.pallas_call(functools.partial(last_kernel, along, halves_of(last), len...  8.85 us
    pallas_call x1, Pallas kernels, per_device(): pl.pallas_call(functools.partial(first_kernel, along), in_specs=[smem] *...  5.29 us
    unnamed x16, local copies, waits for them, and re-layouts  4.52 us
  transfers between devices with their start and end apart: 8, of which 0 were waited for; matrix products, arithmetic and copies ran while one was open for 0% of the time, Pallas kernels for 43%

profile of v3, /device:TPU:6, one launch (start us, length us, event | category | flops | bytes accessed | tf_op | source)
XLA Modules:
  0.0 93.7 jit_solution(3953721952396668392)
XLA Ops:
  0.6 1.5 %pack.1.pairs_ref = bf16[512,128]{1,0:T(8,128)(2,1)} custom-call(bf16[256,128]{1,0:T(8,128)(2,1)} %keys_ref.1, bf16[256,128]{1,0:T(8,128)(2,1)} %values_ref.1), custom_call_target="tpu_custom_call" | custom-call | tf_op jit(solution)/shard_map/pack/pallas_call | solution.py:282
  2.2 10.9 %collective-permute-start = (bf16[512,128]{1,0:T(8,128)(2,1)}, bf16[512,128]{1,0:T(8,128)(2,1)S(1)}, u32[]{:S(2)}, u32[]{:S(2)}) collective-permute-start(bf16[512,128]{1,0:T(8,128)(2,1)} %pack.1.pairs_ref), channel_id=1, source_target_pairs={{0,256},{32,288},{64,320},{96,352},{128,384},{160,416},{192,448},{... | collective-permute-start | bytes 393224 | tf_op jit(solution)/shard_map/ppermute | solution.py:290
  13.1 0.0 copy-start
  13.1 0.9 copy-done
  14.0 0.0 copy-start.1
  14.0 1.2 %copy-done.1 = bf16[4,128,1024]{2,1,0:T(8,128)(2,1)S(1)} copy-done((bf16[4,128,1024]{2,1,0:T(8,128)(2,1)S(1)}, bf16[4,128,1024]{2,1,0:T(8,128)(2,1)}, u32[]{:S(2)}) %copy-start.1) | copy-done | bytes 1048600
  15.2 0.0 copy-start.2
  15.2 1.0 %copy-done.2 = bf16[256,1024]{1,0:T(8,128)(2,1)S(1)} copy-done((bf16[256,1024]{1,0:T(8,128)(2,1)S(1)}, bf16[256,1024]{1,0:T(8,128)(2,1)}, u32[]{:S(2)}) %copy-start.2) | copy-done | bytes 524312
  16.3 0.0 copy-start.4
  16.3 0.7 copy-done.4
  17.0 0.0 copy-start.5
  17.0 0.7 copy-done.5
  17.6 0.0 copy-start.3
  17.6 0.0 copy-start.6
  17.6 5.3 %attend_own.1 = (bf16[256,128]{1,0:T(8,128)(2,1)S(1)}, s32[32,128]{1,0:T(8,128)S(1)}, f32[2,8,128]{2,1,0:T(8,128)S(1)}, f32[9,256,256]{2,1,0:T(8,128)S(1)}, f32[9,256,128]{2,1,0:T(8,128)S(1)}) custom-call(s32[1]{0:T(128)} %bitcast.here_ref, s32[32]{0:T(128)S(1)} %copy-done.5, s32[4,128]{1,0:T(4,128)S(1)} %copy-done.4, bf16[256,1024]{1,0:T(8,128)(2,1)S(1)} %copy-done.2, ...), custom_call_target="tpu_custom_call" | custom-call | flops 2415919104 | bytes 131072 | tf_op jit(solution)/shard_map/attend_own/pallas_call | solution.py:317
  22.9 0.0 collective-permute-done.rest_0_
  23.0 5.4 %collective-permute-start.1 = (bf16[1024,128]{1,0:T(8,128)(2,1)S(1)}, bf16[1024,128]{1,0:T(8,128)(2,1)S(1)}, u32[]{:S(2)}, u32[]{:S(2)}) collective-permute-start(bf16[1024,128]{1,0:T(8,128)(2,1)S(1)} %pad_maximum_fusion.rest_1_), channel_id=1, source_target_pairs={{0,224},{32,0},{64,32},{96,64},{128,96},{160,128},{192,160},{224,1... | collective-permute-start | bytes 786440 | tf_op jit(solution)/shard_map/ppermute | solution.py:279
  28.3 1.9 %collective-permute-start.2 = (bf16[1024,128]{1,0:T(8,128)(2,1)S(1)}, bf16[1024,128]{1,0:T(8,128)(2,1)S(1)}, u32[]{:S(2)}, u32[]{:S(2)}) collective-permute-start(bf16[1024,128]{1,0:T(8,128)(2,1)S(1)} %pad_maximum_fusion.rest_1_), channel_id=1, source_target_pairs={{0,32},{32,64},{64,96},{96,128},{128,160},{160,192},{192,224},{224... | collective-permute-start | bytes 786440 | tf_op jit(solution)/shard_map/ppermute | solution.py:279
  30.3 0.0 copy-done.3
  30.3 0.0 copy-done.6
  30.3 5.3 %attend_other.1 = (f32[2,8,128]{2,1,0:T(8,128)S(1)}, f32[9,256,256]{2,1,0:T(8,128)S(1)}, f32[9,256,128]{2,1,0:T(8,128)S(1)}) custom-call(s32[1]{0:T(128)} %bitcast.here_ref, s32[32]{0:T(128)S(1)} %copy-done.6, bf16[256,1024]{1,0:T(8,128)(2,1)S(1)} %copy-done.3, bf16[256,128]{1,0:T(8,128)(2,1)S(1)} %get-tuple-element.21.dec_query_ref, ...), custom_call_target="tpu_custom_call" | custom-call | flops 9663676416 | bytes 524288 | tf_op jit(solution)/shard_map/attend_other/pallas_call | solution.py:330
  35.6 0.0 collective-permute-done.1.rest_0_.rest_2_
  35.6 5.1 %collective-permute-start.3 = (bf16[1024,128]{1,0:T(8,128)(2,1)S(1)}, bf16[1024,128]{1,0:T(8,128)(2,1)S(1)}, u32[]{:S(2)}, u32[]{:S(2)}) collective-permute-start(bf16[1024,128]{1,0:T(8,128)(2,1)S(1)} %collective-permute-done.1.rest_0_.rest_2_), channel_id=1, source_target_pairs={{0,224},{32,0},{64,32},{96,64},{128,96},{160,128},{192,160},{224,1... | collective-permute-start | bytes 786440 | tf_op jit(solution)/shard_map/ppermute | solution.py:279
  40.7 0.0 collective-permute-done.2.rest_1_.rest_3_
  40.7 1.9 %collective-permute-start.4 = (bf16[1024,128]{1,0:T(8,128)(2,1)S(1)}, bf16[1024,128]{1,0:T(8,128)(2,1)S(1)}, u32[]{:S(2)}, u32[]{:S(2)}) collective-permute-start(bf16[1024,128]{1,0:T(8,128)(2,1)S(1)} %collective-permute-done.2.rest_1_.rest_3_), channel_id=1, source_target_pairs={{0,32},{32,64},{64,96},{96,128},{128,160},{160,192},{192,224},{224... | collective-permute-start | bytes 786440 | tf_op jit(solution)/shard_map/ppermute | solution.py:279
  42.7 9.8 %attend_0.1 = (f32[2,8,128]{2,1,0:T(8,128)S(1)}, f32[9,256,256]{2,1,0:T(8,128)S(1)}, f32[9,256,128]{2,1,0:T(8,128)S(1)}) custom-call(s32[1]{0:T(128)} %bitcast.here_ref, s32[32]{0:T(128)S(1)} %copy-done.6, bf16[256,1024]{1,0:T(8,128)(2,1)S(1)} %copy-done.3, bf16[256,128]{1,0:T(8,128)(2,1)S(1)} %get-tuple-element.21.dec_query_ref, ...), custom_call_target="tpu_custom_call" | custom-call | flops 9663676416 | bytes 524288 | tf_op jit(solution)/shard_map/attend_0/pallas_call | solution.py:330
  52.5 0.0 collective-permute-done.3.rest_0_.rest_4_
  52.5 5.1 %collective-permute-start.5 = (bf16[1024,128]{1,0:T(8,128)(2,1)S(1)}, bf16[1024,128]{1,0:T(8,128)(2,1)S(1)}, u32[]{:S(2)}, u32[]{:S(2)}) collective-permute-start(bf16[1024,128]{1,0:T(8,128)(2,1)S(1)} %collective-permute-done.3.rest_0_.rest_4_), channel_id=1, source_target_pairs={{0,224},{32,0},{64,32},{96,64},{128,96},{160,128},{192,160},{224,1... | collective-permute-start | bytes 786440 | tf_op jit(solution)/shard_map/ppermute | solution.py:279
  57.7 0.0 collective-permute-done.4.rest_1_.rest_5_
  57.7 1.9 %collective-permute-start.6 = (bf16[1024,128]{1,0:T(8,128)(2,1)S(1)}, bf16[1024,128]{1,0:T(8,128)(2,1)S(1)}, u32[]{:S(2)}, u32[]{:S(2)}) collective-permute-start(bf16[1024,128]{1,0:T(8,128)(2,1)S(1)} %collective-permute-done.4.rest_1_.rest_5_), channel_id=1, source_target_pairs={{0,32},{32,64},{64,96},{96,128},{128,160},{160,192},{192,224},{224... | collective-permute-start | bytes 786440 | tf_op jit(solution)/shard_map/ppermute | solution.py:279
  59.6 9.8 %attend_1.1 = (f32[2,8,128]{2,1,0:T(8,128)S(1)}, f32[9,256,256]{2,1,0:T(8,128)S(1)}, f32[9,256,128]{2,1,0:T(8,128)S(1)}) custom-call(s32[1]{0:T(128)} %bitcast.here_ref, s32[32]{0:T(128)S(1)} %copy-done.6, bf16[256,1024]{1,0:T(8,128)(2,1)S(1)} %copy-done.3, bf16[256,128]{1,0:T(8,128)(2,1)S(1)} %get-tuple-element.21.dec_query_ref, ...), custom_call_target="tpu_custom_call" | custom-call | flops 9663676416 | bytes 524288 | tf_op jit(solution)/shard_map/attend_1/pallas_call | solution.py:330
  69.5 0.0 collective-permute-done.5.rest_0_.rest_6_
  69.5 5.3 %collective-permute-start.7 = (bf16[1024,128]{1,0:T(8,128)(2,1)S(1)}, bf16[1024,128]{1,0:T(8,128)(2,1)S(1)}, u32[]{:S(2)}, u32[]{:S(2)}) collective-permute-start(bf16[1024,128]{1,0:T(8,128)(2,1)S(1)} %collective-permute-done.5.rest_0_.rest_6_), channel_id=1, source_target_pairs={{0,224},{32,0},{64,32},{96,64},{128,96},{160,128},{192,160},{224,1... | collective-permute-start | bytes 786440 | tf_op jit(solution)/shard_map/ppermute | solution.py:279
  74.8 0.0 collective-permute-done.6.rest_1_.rest_7_
  74.8 0.0 copy-start.7
  74.8 9.8 %attend_2.1 = (f32[2,8,128]{2,1,0:T(8,128)S(1)}, f32[9,256,256]{2,1,0:T(8,128)S(1)}, f32[9,256,128]{2,1,0:T(8,128)S(1)}) custom-call(s32[1]{0:T(128)} %bitcast.here_ref, s32[32]{0:T(128)S(1)} %copy-done.6, bf16[256,1024]{1,0:T(8,128)(2,1)S(1)} %copy-done.3, bf16[256,128]{1,0:T(8,128)(2,1)S(1)} %get-tuple-element.21.dec_query_ref, ...), custom_call_target="tpu_custom_call" | custom-call | flops 9663676416 | bytes 524288 | tf_op jit(solution)/shard_map/attend_2/pallas_call | solution.py:330
  84.7 0.0 collective-permute-done.7.rest_0_.rest_8_
  84.7 0.0 copy-done.7
  84.7 8.9 %attend_last.1 = (bf16[256,1024]{1,0:T(8,128)(2,1)}, bf16[256,128]{1,0:T(8,128)(2,1)}, bf16[256,128]{1,0:T(8,128)(2,1)}, bf16[4,8,1024]{2,1,0:T(8,128)(2,1)}) custom-call(s32[1]{0:T(128)} %bitcast.here_ref, s32[32]{0:T(128)S(1)} %copy-done.6, s32[16]{0:T(128)S(1)} %copy-done.7, bf16[256,1024]{1,0:T(8,128)(2,1)S(1)} %copy-done.3, ...), custom_call_target="tpu_custom_call" | custom-call | flops 4831838208 | bytes 262144 | tf_op jit(solution)/shard_map/attend_last/pallas_call | solution.py:349
  (1 shorter events, 0.0 us)
Async XLA Ops:
  2.2 20.7 %collective-permute-start = (bf16[512,128]{1,0:T(8,128)(2,1)}, bf16[512,128]{1,0:T(8,128)(2,1)S(1)}, u32[]{:S(2)}, u32[]{:S(2)}) collective-permute-start(bf16[512,128]{1,0:T(8,128)(2,1)} %pack.1.pairs_ref), channel_id=1, source_target_pairs={{0,256},{32,288},{64,320},{96,352},{128,384},{160,416},{192,448},{... | collective-permute-start | bytes 393224 | tf_op jit(solution)/shard_map/ppermute | solution.py:290
  13.1 0.9 copy-start
  14.0 1.2 %copy-start.1 = (bf16[4,128,1024]{2,1,0:T(8,128)(2,1)S(1)}, bf16[4,128,1024]{2,1,0:T(8,128)(2,1)}, u32[]{:S(2)}) copy-start(bf16[4,128,1024]{2,1,0:T(8,128)(2,1)} %dec_ref.1) | copy-start | bytes 3145732
  15.2 1.0 %copy-start.2 = (bf16[256,1024]{1,0:T(8,128)(2,1)S(1)}, bf16[256,1024]{1,0:T(8,128)(2,1)}, u32[]{:S(2)}) copy-start(bf16[256,1024]{1,0:T(8,128)(2,1)} %query_ref.11) | copy-start | bytes 1572868
  16.3 0.7 copy-start.4
  17.0 0.7 copy-start.5
  17.6 12.7 %copy-start.3 = (bf16[256,1024]{1,0:T(8,128)(2,1)S(1)}, bf16[256,1024]{1,0:T(8,128)(2,1)}, u32[]{:S(2)}) copy-start(bf16[256,1024]{1,0:T(8,128)(2,1)} %query_ref.11) | copy-start | bytes 1572868
  17.6 12.7 %copy-start.6 = (s32[32]{0:T(128)S(1)}, s32[32]{0:T(128)}, u32[]{:S(2)}) copy-start(s32[32]{0:T(128)} %order_ref.11) | copy-start | bytes 388
  23.0 12.6 %collective-permute-start.1 = (bf16[1024,128]{1,0:T(8,128)(2,1)S(1)}, bf16[1024,128]{1,0:T(8,128)(2,1)S(1)}, u32[]{:S(2)}, u32[]{:S(2)}) collective-permute-start(bf16[1024,128]{1,0:T(8,128)(2,1)S(1)} %pad_maximum_fusion.rest_1_), channel_id=1, source_target_pairs={{0,224},{32,0},{64,32},{96,64},{128,96},{160,128},{192,160},{224,1... | collective-permute-start | bytes 786440 | tf_op jit(solution)/shard_map/ppermute | solution.py:279
  28.3 12.4 %collective-permute-start.2 = (bf16[1024,128]{1,0:T(8,128)(2,1)S(1)}, bf16[1024,128]{1,0:T(8,128)(2,1)S(1)}, u32[]{:S(2)}, u32[]{:S(2)}) collective-permute-start(bf16[1024,128]{1,0:T(8,128)(2,1)S(1)} %pad_maximum_fusion.rest_1_), channel_id=1, source_target_pairs={{0,32},{32,64},{64,96},{96,128},{128,160},{160,192},{192,224},{224... | collective-permute-start | bytes 786440 | tf_op jit(solution)/shard_map/ppermute | solution.py:279
  35.6 16.9 %collective-permute-start.3 = (bf16[1024,128]{1,0:T(8,128)(2,1)S(1)}, bf16[1024,128]{1,0:T(8,128)(2,1)S(1)}, u32[]{:S(2)}, u32[]{:S(2)}) collective-permute-start(bf16[1024,128]{1,0:T(8,128)(2,1)S(1)} %collective-permute-done.1.rest_0_.rest_2_), channel_id=1, source_target_pairs={{0,224},{32,0},{64,32},{96,64},{128,96},{160,128},{192,160},{224,1... | collective-permute-start | bytes 786440 | tf_op jit(solution)/shard_map/ppermute | solution.py:279
  40.7 16.9 %collective-permute-start.4 = (bf16[1024,128]{1,0:T(8,128)(2,1)S(1)}, bf16[1024,128]{1,0:T(8,128)(2,1)S(1)}, u32[]{:S(2)}, u32[]{:S(2)}) collective-permute-start(bf16[1024,128]{1,0:T(8,128)(2,1)S(1)} %collective-permute-done.2.rest_1_.rest_3_), channel_id=1, source_target_pairs={{0,32},{32,64},{64,96},{96,128},{128,160},{160,192},{192,224},{224... | collective-permute-start | bytes 786440 | tf_op jit(solution)/shard_map/ppermute | solution.py:279
  52.5 16.9 %collective-permute-start.5 = (bf16[1024,128]{1,0:T(8,128)(2,1)S(1)}, bf16[1024,128]{1,0:T(8,128)(2,1)S(1)}, u32[]{:S(2)}, u32[]{:S(2)}) collective-permute-start(bf16[1024,128]{1,0:T(8,128)(2,1)S(1)} %collective-permute-done.3.rest_0_.rest_4_), channel_id=1, source_target_pairs={{0,224},{32,0},{64,32},{96,64},{128,96},{160,128},{192,160},{224,1... | collective-permute-start | bytes 786440 | tf_op jit(solution)/shard_map/ppermute | solution.py:279
  57.7 17.1 %collective-permute-start.6 = (bf16[1024,128]{1,0:T(8,128)(2,1)S(1)}, bf16[1024,128]{1,0:T(8,128)(2,1)S(1)}, u32[]{:S(2)}, u32[]{:S(2)}) collective-permute-start(bf16[1024,128]{1,0:T(8,128)(2,1)S(1)} %collective-permute-done.4.rest_1_.rest_5_), channel_id=1, source_target_pairs={{0,32},{32,64},{64,96},{96,128},{128,160},{160,192},{192,224},{224... | collective-permute-start | bytes 786440 | tf_op jit(solution)/shard_map/ppermute | solution.py:279
  69.5 15.2 %collective-permute-start.7 = (bf16[1024,128]{1,0:T(8,128)(2,1)S(1)}, bf16[1024,128]{1,0:T(8,128)(2,1)S(1)}, u32[]{:S(2)}, u32[]{:S(2)}) collective-permute-start(bf16[1024,128]{1,0:T(8,128)(2,1)S(1)} %collective-permute-done.5.rest_0_.rest_6_), channel_id=1, source_target_pairs={{0,224},{32,0},{64,32},{96,64},{128,96},{160,128},{192,160},{224,1... | collective-permute-start | bytes 786440 | tf_op jit(solution)/shard_map/ppermute | solution.py:279
  74.8 9.9 %copy-start.7 = (s32[16]{0:T(128)S(1)}, s32[16]{0:T(128)}, u32[]{:S(2)}) copy-start(s32[16]{0:T(128)} %owner_ref.1) | copy-start | bytes 196

commit v4 on v3

--- a/solution.py
+++ b/solution.py
@@ -283,7 +283,7 @@
         pack_kernel,
         in_specs=[pl.BlockSpec(memory_space=pl.ANY)] * 2,
         out_specs=pl.BlockSpec(memory_space=pltpu.VMEM),
-        out_shape=jax.ShapeDtypeStruct((2 * rows, HD), keys.dtype),
+        out_shape=pltpu.VMEM((2 * rows, HD), keys.dtype),
         scratch_shapes=[pltpu.SemaphoreType.DMA((2,))],
         name="pack",
     )(keys, values)

time: 94.2 us -> 92.7 us (0.984)
    unnamed x16 -> x14, local copies, waits for them, and re-layouts: 4.52 us -> 3.61 us
  transfers between devices with their start and end apart: 8 -> 8, of which waited for: 0 -> 0; matrix products, arithmetic and copies ran while one was open for 0% -> 0% of each run, Pallas kernels for 43% -> 44%
where the time goes in v4:
time: 92.7 us; the launch traced here: 92.3 us
  Pallas kernels  50 us (54%)
  starting transfers between devices  37.6 us (41%)
  local copies, waits for them, and re-layouts  3.61 us (4%)
  between operations  1.02 us (1%)
    pallas_call x4, Pallas kernels, attend_more(): pl.pallas_call(functools.partial(next_kernel, along, places_of, len(block...  34.9 us
    ppermute x7, starting transfers between devices, shift(): return lax.ppermute(block, 'ctx', moves)  26.7 us
    ppermute x1, starting transfers between devices, per_device(): other = lax.ppermute(own, 'ctx', swap)  10.9 us
    pallas_call x1, Pallas kernels, per_device(): pl.pallas_call(functools.partial(last_kernel, along, halves_of(last), len...  8.9 us
    pallas_call x1, Pallas kernels, per_device(): pl.pallas_call(functools.partial(first_kernel, along), in_specs=[smem] *...  5.3 us
    unnamed x14, local copies, waits for them, and re-layouts  3.61 us
  transfers between devices with their start and end apart: 8, of which 0 were waited for; matrix products, arithmetic and copies ran while one was open for 0% of the time, Pallas kernels for 44%

profile of v4, /device:TPU:6, one launch (start us, length us, event | category | flops | bytes accessed | tf_op | source)
XLA Modules:
  0.0 92.3 jit_solution(1943649573726396417)
XLA Ops:
  0.6 0.9 pack.1.pairs_ref
  1.5 10.9 %collective-permute-start = (bf16[512,128]{1,0:T(8,128)(2,1)S(1)}, bf16[512,128]{1,0:T(8,128)(2,1)S(1)}, u32[]{:S(2)}, u32[]{:S(2)}) collective-permute-start(bf16[512,128]{1,0:T(8,128)(2,1)S(1)} %pack.1.pairs_ref), channel_id=1, source_target_pairs={{0,256},{32,288},{64,320},{96,352},{128,384},{160,416},{192,448},{... | collective-permute-start | bytes 393224 | tf_op jit(solution)/shard_map/ppermute | solution.py:290
  12.5 0.0 copy-start
  12.5 1.2 %copy-done = bf16[4,128,1024]{2,1,0:T(8,128)(2,1)S(1)} copy-done((bf16[4,128,1024]{2,1,0:T(8,128)(2,1)S(1)}, bf16[4,128,1024]{2,1,0:T(8,128)(2,1)}, u32[]{:S(2)}) %copy-start) | copy-done | bytes 1048600
  13.7 0.0 copy-start.1
  13.7 1.0 %copy-done.1 = bf16[256,1024]{1,0:T(8,128)(2,1)S(1)} copy-done((bf16[256,1024]{1,0:T(8,128)(2,1)S(1)}, bf16[256,1024]{1,0:T(8,128)(2,1)}, u32[]{:S(2)}) %copy-start.1) | copy-done | bytes 524312
  14.7 0.0 copy-start.3
  14.7 0.7 copy-done.3
  15.4 0.0 copy-start.4
  15.4 0.7 copy-done.4
  16.1 0.0 copy-start.2
  16.1 0.0 copy-start.5
  16.1 5.3 %attend_own.1 = (bf16[256,128]{1,0:T(8,128)(2,1)S(1)}, s32[32,128]{1,0:T(8,128)S(1)}, f32[2,8,128]{2,1,0:T(8,128)S(1)}, f32[9,256,256]{2,1,0:T(8,128)S(1)}, f32[9,256,128]{2,1,0:T(8,128)S(1)}) custom-call(s32[1]{0:T(128)} %bitcast.here_ref, s32[32]{0:T(128)S(1)} %copy-done.4, s32[4,128]{1,0:T(4,128)S(1)} %copy-done.3, bf16[256,1024]{1,0:T(8,128)(2,1)S(1)} %copy-done.1, ...), custom_call_target="tpu_custom_call" | custom-call | flops 2415919104 | bytes 131072 | tf_op jit(solution)/shard_map/attend_own/pallas_call | solution.py:317
  21.4 0.0 collective-permute-done.rest_0_
  21.4 5.4 %collective-permute-start.1 = (bf16[1024,128]{1,0:T(8,128)(2,1)S(1)}, bf16[1024,128]{1,0:T(8,128)(2,1)S(1)}, u32[]{:S(2)}, u32[]{:S(2)}) collective-permute-start(bf16[1024,128]{1,0:T(8,128)(2,1)S(1)} %pad_maximum_fusion.rest_1_), channel_id=1, source_target_pairs={{0,224},{32,0},{64,32},{96,64},{128,96},{160,128},{192,160},{224,1... | collective-permute-start | bytes 786440 | tf_op jit(solution)/shard_map/ppermute | solution.py:279
  26.8 1.9 %collective-permute-start.2 = (bf16[1024,128]{1,0:T(8,128)(2,1)S(1)}, bf16[1024,128]{1,0:T(8,128)(2,1)S(1)}, u32[]{:S(2)}, u32[]{:S(2)}) collective-permute-start(bf16[1024,128]{1,0:T(8,128)(2,1)S(1)} %pad_maximum_fusion.rest_1_), channel_id=1, source_target_pairs={{0,32},{32,64},{64,96},{96,128},{128,160},{160,192},{192,224},{224... | collective-permute-start | bytes 786440 | tf_op jit(solution)/shard_map/ppermute | solution.py:279
  28.7 0.0 copy-done.2
  28.7 0.0 copy-done.5
  28.7 5.3 %attend_other.1 = (f32[2,8,128]{2,1,0:T(8,128)S(1)}, f32[9,256,256]{2,1,0:T(8,128)S(1)}, f32[9,256,128]{2,1,0:T(8,128)S(1)}) custom-call(s32[1]{0:T(128)} %bitcast.here_ref, s32[32]{0:T(128)S(1)} %copy-done.5, bf16[256,1024]{1,0:T(8,128)(2,1)S(1)} %copy-done.2, bf16[256,128]{1,0:T(8,128)(2,1)S(1)} %get-tuple-element.21.dec_query_ref, ...), custom_call_target="tpu_custom_call" | custom-call | flops 9663676416 | bytes 524288 | tf_op jit(solution)/shard_map/attend_other/pallas_call | solution.py:330
  34.0 0.0 collective-permute-done.1.rest_0_.rest_2_
  34.0 5.1 %collective-permute-start.3 = (bf16[1024,128]{1,0:T(8,128)(2,1)S(1)}, bf16[1024,128]{1,0:T(8,128)(2,1)S(1)}, u32[]{:S(2)}, u32[]{:S(2)}) collective-permute-start(bf16[1024,128]{1,0:T(8,128)(2,1)S(1)} %collective-permute-done.1.rest_0_.rest_2_), channel_id=1, source_target_pairs={{0,224},{32,0},{64,32},{96,64},{128,96},{160,128},{192,160},{224,1... | collective-permute-start | bytes 786440 | tf_op jit(solution)/shard_map/ppermute | solution.py:279
  39.2 0.0 collective-permute-done.2.rest_1_.rest_3_
  39.2 1.9 %collective-permute-start.4 = (bf16[1024,128]{1,0:T(8,128)(2,1)S(1)}, bf16[1024,128]{1,0:T(8,128)(2,1)S(1)}, u32[]{:S(2)}, u32[]{:S(2)}) collective-permute-start(bf16[1024,128]{1,0:T(8,128)(2,1)S(1)} %collective-permute-done.2.rest_1_.rest_3_), channel_id=1, source_target_pairs={{0,32},{32,64},{64,96},{96,128},{128,160},{160,192},{192,224},{224... | collective-permute-start | bytes 786440 | tf_op jit(solution)/shard_map/ppermute | solution.py:279
  41.1 9.8 %attend_0.1 = (f32[2,8,128]{2,1,0:T(8,128)S(1)}, f32[9,256,256]{2,1,0:T(8,128)S(1)}, f32[9,256,128]{2,1,0:T(8,128)S(1)}) custom-call(s32[1]{0:T(128)} %bitcast.here_ref, s32[32]{0:T(128)S(1)} %copy-done.5, bf16[256,1024]{1,0:T(8,128)(2,1)S(1)} %copy-done.2, bf16[256,128]{1,0:T(8,128)(2,1)S(1)} %get-tuple-element.21.dec_query_ref, ...), custom_call_target="tpu_custom_call" | custom-call | flops 9663676416 | bytes 524288 | tf_op jit(solution)/shard_map/attend_0/pallas_call | solution.py:330
  51.0 0.0 collective-permute-done.3.rest_0_.rest_4_
  51.0 5.1 %collective-permute-start.5 = (bf16[1024,128]{1,0:T(8,128)(2,1)S(1)}, bf16[1024,128]{1,0:T(8,128)(2,1)S(1)}, u32[]{:S(2)}, u32[]{:S(2)}) collective-permute-start(bf16[1024,128]{1,0:T(8,128)(2,1)S(1)} %collective-permute-done.3.rest_0_.rest_4_), channel_id=1, source_target_pairs={{0,224},{32,0},{64,32},{96,64},{128,96},{160,128},{192,160},{224,1... | collective-permute-start | bytes 786440 | tf_op jit(solution)/shard_map/ppermute | solution.py:279
  56.1 0.0 collective-permute-done.4.rest_1_.rest_5_
  56.1 1.9 %collective-permute-start.6 = (bf16[1024,128]{1,0:T(8,128)(2,1)S(1)}, bf16[1024,128]{1,0:T(8,128)(2,1)S(1)}, u32[]{:S(2)}, u32[]{:S(2)}) collective-permute-start(bf16[1024,128]{1,0:T(8,128)(2,1)S(1)} %collective-permute-done.4.rest_1_.rest_5_), channel_id=1, source_target_pairs={{0,32},{32,64},{64,96},{96,128},{128,160},{160,192},{192,224},{224... | collective-permute-start | bytes 786440 | tf_op jit(solution)/shard_map/ppermute | solution.py:279
  58.1 9.9 %attend_1.1 = (f32[2,8,128]{2,1,0:T(8,128)S(1)}, f32[9,256,256]{2,1,0:T(8,128)S(1)}, f32[9,256,128]{2,1,0:T(8,128)S(1)}) custom-call(s32[1]{0:T(128)} %bitcast.here_ref, s32[32]{0:T(128)S(1)} %copy-done.5, bf16[256,1024]{1,0:T(8,128)(2,1)S(1)} %copy-done.2, bf16[256,128]{1,0:T(8,128)(2,1)S(1)} %get-tuple-element.21.dec_query_ref, ...), custom_call_target="tpu_custom_call" | custom-call | flops 9663676416 | bytes 524288 | tf_op jit(solution)/shard_map/attend_1/pallas_call | solution.py:330
  68.0 0.0 collective-permute-done.5.rest_0_.rest_6_
  68.0 5.3 %collective-permute-start.7 = (bf16[1024,128]{1,0:T(8,128)(2,1)S(1)}, bf16[1024,128]{1,0:T(8,128)(2,1)S(1)}, u32[]{:S(2)}, u32[]{:S(2)}) collective-permute-start(bf16[1024,128]{1,0:T(8,128)(2,1)S(1)} %collective-permute-done.5.rest_0_.rest_6_), channel_id=1, source_target_pairs={{0,224},{32,0},{64,32},{96,64},{128,96},{160,128},{192,160},{224,1... | collective-permute-start | bytes 786440 | tf_op jit(solution)/shard_map/ppermute | solution.py:279
  73.3 0.0 collective-permute-done.6.rest_1_.rest_7_
  73.3 0.0 copy-start.6
  73.3 9.8 %attend_2.1 = (f32[2,8,128]{2,1,0:T(8,128)S(1)}, f32[9,256,256]{2,1,0:T(8,128)S(1)}, f32[9,256,128]{2,1,0:T(8,128)S(1)}) custom-call(s32[1]{0:T(128)} %bitcast.here_ref, s32[32]{0:T(128)S(1)} %copy-done.5, bf16[256,1024]{1,0:T(8,128)(2,1)S(1)} %copy-done.2, bf16[256,128]{1,0:T(8,128)(2,1)S(1)} %get-tuple-element.21.dec_query_ref, ...), custom_call_target="tpu_custom_call" | custom-call | flops 9663676416 | bytes 524288 | tf_op jit(solution)/shard_map/attend_2/pallas_call | solution.py:330
  83.2 0.0 collective-permute-done.7.rest_0_.rest_8_
  83.2 0.0 copy-done.6
  83.2 8.9 %attend_last.1 = (bf16[256,1024]{1,0:T(8,128)(2,1)}, bf16[256,128]{1,0:T(8,128)(2,1)}, bf16[256,128]{1,0:T(8,128)(2,1)}, bf16[4,8,1024]{2,1,0:T(8,128)(2,1)}) custom-call(s32[1]{0:T(128)} %bitcast.here_ref, s32[32]{0:T(128)S(1)} %copy-done.5, s32[16]{0:T(128)S(1)} %copy-done.6, bf16[256,1024]{1,0:T(8,128)(2,1)S(1)} %copy-done.2, ...), custom_call_target="tpu_custom_call" | custom-call | flops 4831838208 | bytes 262144 | tf_op jit(solution)/shard_map/attend_last/pallas_call | solution.py:349
  (1 shorter events, 0.0 us)
Async XLA Ops:
  1.5 19.9 %collective-permute-start = (bf16[512,128]{1,0:T(8,128)(2,1)S(1)}, bf16[512,128]{1,0:T(8,128)(2,1)S(1)}, u32[]{:S(2)}, u32[]{:S(2)}) collective-permute-start(bf16[512,128]{1,0:T(8,128)(2,1)S(1)} %pack.1.pairs_ref), channel_id=1, source_target_pairs={{0,256},{32,288},{64,320},{96,352},{128,384},{160,416},{192,448},{... | collective-permute-start | bytes 393224 | tf_op jit(solution)/shard_map/ppermute | solution.py:290
  12.5 1.2 %copy-start = (bf16[4,128,1024]{2,1,0:T(8,128)(2,1)S(1)}, bf16[4,128,1024]{2,1,0:T(8,128)(2,1)}, u32[]{:S(2)}) copy-start(bf16[4,128,1024]{2,1,0:T(8,128)(2,1)} %dec_ref.1) | copy-start | bytes 3145732
  13.7 1.0 %copy-start.1 = (bf16[256,1024]{1,0:T(8,128)(2,1)S(1)}, bf16[256,1024]{1,0:T(8,128)(2,1)}, u32[]{:S(2)}) copy-start(bf16[256,1024]{1,0:T(8,128)(2,1)} %query_ref.11) | copy-start | bytes 1572868
  14.7 0.7 copy-start.3
  15.4 0.7 copy-start.4
  16.1 12.7 %copy-start.2 = (bf16[256,1024]{1,0:T(8,128)(2,1)S(1)}, bf16[256,1024]{1,0:T(8,128)(2,1)}, u32[]{:S(2)}) copy-start(bf16[256,1024]{1,0:T(8,128)(2,1)} %query_ref.11) | copy-start | bytes 1572868
  16.1 12.7 %copy-start.5 = (s32[32]{0:T(128)S(1)}, s32[32]{0:T(128)}, u32[]{:S(2)}) copy-start(s32[32]{0:T(128)} %order_ref.11) | copy-start | bytes 388
  21.4 12.6 %collective-permute-start.1 = (bf16[1024,128]{1,0:T(8,128)(2,1)S(1)}, bf16[1024,128]{1,0:T(8,128)(2,1)S(1)}, u32[]{:S(2)}, u32[]{:S(2)}) collective-permute-start(bf16[1024,128]{1,0:T(8,128)(2,1)S(1)} %pad_maximum_fusion.rest_1_), channel_id=1, source_target_pairs={{0,224},{32,0},{64,32},{96,64},{128,96},{160,128},{192,160},{224,1... | collective-permute-start | bytes 786440 | tf_op jit(solution)/shard_map/ppermute | solution.py:279
  26.8 12.4 %collective-permute-start.2 = (bf16[1024,128]{1,0:T(8,128)(2,1)S(1)}, bf16[1024,128]{1,0:T(8,128)(2,1)S(1)}, u32[]{:S(2)}, u32[]{:S(2)}) collective-permute-start(bf16[1024,128]{1,0:T(8,128)(2,1)S(1)} %pad_maximum_fusion.rest_1_), channel_id=1, source_target_pairs={{0,32},{32,64},{64,96},{96,128},{128,160},{160,192},{192,224},{224... | collective-permute-start | bytes 786440 | tf_op jit(solution)/shard_map/ppermute | solution.py:279
  34.0 16.9 %collective-permute-start.3 = (bf16[1024,128]{1,0:T(8,128)(2,1)S(1)}, bf16[1024,128]{1,0:T(8,128)(2,1)S(1)}, u32[]{:S(2)}, u32[]{:S(2)}) collective-permute-start(bf16[1024,128]{1,0:T(8,128)(2,1)S(1)} %collective-permute-done.1.rest_0_.rest_2_), channel_id=1, source_target_pairs={{0,224},{32,0},{64,32},{96,64},{128,96},{160,128},{192,160},{224,1... | collective-permute-start | bytes 786440 | tf_op jit(solution)/shard_map/ppermute | solution.py:279
  39.2 16.9 %collective-permute-start.4 = (bf16[1024,128]{1,0:T(8,128)(2,1)S(1)}, bf16[1024,128]{1,0:T(8,128)(2,1)S(1)}, u32[]{:S(2)}, u32[]{:S(2)}) collective-permute-start(bf16[1024,128]{1,0:T(8,128)(2,1)S(1)} %collective-permute-done.2.rest_1_.rest_3_), channel_id=1, source_target_pairs={{0,32},{32,64},{64,96},{96,128},{128,160},{160,192},{192,224},{224... | collective-permute-start | bytes 786440 | tf_op jit(solution)/shard_map/ppermute | solution.py:279
  51.0 17.0 %collective-permute-start.5 = (bf16[1024,128]{1,0:T(8,128)(2,1)S(1)}, bf16[1024,128]{1,0:T(8,128)(2,1)S(1)}, u32[]{:S(2)}, u32[]{:S(2)}) collective-permute-start(bf16[1024,128]{1,0:T(8,128)(2,1)S(1)} %collective-permute-done.3.rest_0_.rest_4_), channel_id=1, source_target_pairs={{0,224},{32,0},{64,32},{96,64},{128,96},{160,128},{192,160},{224,1... | collective-permute-start | bytes 786440 | tf_op jit(solution)/shard_map/ppermute | solution.py:279
  56.1 17.2 %collective-permute-start.6 = (bf16[1024,128]{1,0:T(8,128)(2,1)S(1)}, bf16[1024,128]{1,0:T(8,128)(2,1)S(1)}, u32[]{:S(2)}, u32[]{:S(2)}) collective-permute-start(bf16[1024,128]{1,0:T(8,128)(2,1)S(1)} %collective-permute-done.4.rest_1_.rest_5_), channel_id=1, source_target_pairs={{0,32},{32,64},{64,96},{96,128},{128,160},{160,192},{192,224},{224... | collective-permute-start | bytes 786440 | tf_op jit(solution)/shard_map/ppermute | solution.py:279
  68.0 15.2 %collective-permute-start.7 = (bf16[1024,128]{1,0:T(8,128)(2,1)S(1)}, bf16[1024,128]{1,0:T(8,128)(2,1)S(1)}, u32[]{:S(2)}, u32[]{:S(2)}) collective-permute-start(bf16[1024,128]{1,0:T(8,128)(2,1)S(1)} %collective-permute-done.5.rest_0_.rest_6_), channel_id=1, source_target_pairs={{0,224},{32,0},{64,32},{96,64},{128,96},{160,128},{192,160},{224,1... | collective-permute-start | bytes 786440 | tf_op jit(solution)/shard_map/ppermute | solution.py:279
  73.3 9.9 %copy-start.6 = (s32[16]{0:T(128)S(1)}, s32[16]{0:T(128)}, u32[]{:S(2)}) copy-start(s32[16]{0:T(128)} %owner_ref.1) | copy-start | bytes 196

commit v5 on v4

--- a/solution.py
+++ b/solution.py
@@ -67,7 +67,7 @@
     def start_sums(group):
         return jnp.zeros((rows, 2 * HD), jnp.float32) if sums_ref is None else sums_ref[group]
 
-    for group in range(groups):
+    for group in [heads, *range(heads)]:
         row_places = query_places if group < heads else dec_places
         query = query_ref[:, group * HD : (group + 1) * HD] if group < heads else dec_query_ref[...]
         sums = start_sums(group)

time: 92.7 us -> 92.7 us (level)
  no operation moved by 1% of the time
where the time goes in v5:
time: 92.7 us; the launch traced here: 92.2 us
  Pallas kernels  49.9 us (54%)
  starting transfers between devices  37.6 us (41%)
  local copies, waits for them, and re-layouts  3.61 us (4%)
  between operations  1.02 us (1%)
    pallas_call x4, Pallas kernels, attend_more(): pl.pallas_call(functools.partial(next_kernel, along, places_of, len(block...  34.8 us
    ppermute x7, starting transfers between devices, shift(): return lax.ppermute(block, 'ctx', moves)  26.7 us
    ppermute x1, starting transfers between devices, per_device(): other = lax.ppermute(own, 'ctx', swap)  10.9 us
    pallas_call x1, Pallas kernels, per_device(): pl.pallas_call(functools.partial(last_kernel, along, halves_of(last), len...  8.9 us
    pallas_call x1, Pallas kernels, per_device(): pl.pallas_call(functools.partial(first_kernel, along), in_specs=[smem] *...  5.3 us
    unnamed x14, local copies, waits for them, and re-layouts  3.61 us
  transfers between devices with their start and end apart: 8, of which 0 were waited for; matrix products, arithmetic and copies ran while one was open for 0% of the time, Pallas kernels for 44%

profile of v5, /device:TPU:6, one launch (start us, length us, event | category | flops | bytes accessed | tf_op | source)
XLA Modules:
  0.0 92.2 jit_solution(15861206748773642897)
XLA Ops:
  0.6 0.9 pack.1.pairs_ref
  1.5 10.9 %collective-permute-start = (bf16[512,128]{1,0:T(8,128)(2,1)S(1)}, bf16[512,128]{1,0:T(8,128)(2,1)S(1)}, u32[]{:S(2)}, u32[]{:S(2)}) collective-permute-start(bf16[512,128]{1,0:T(8,128)(2,1)S(1)} %pack.1.pairs_ref), channel_id=1, source_target_pairs={{0,256},{32,288},{64,320},{96,352},{128,384},{160,416},{192,448},{... | collective-permute-start | bytes 393224 | tf_op jit(solution)/shard_map/ppermute | solution.py:290
  12.5 0.0 copy-start
  12.5 1.2 %copy-done = bf16[4,128,1024]{2,1,0:T(8,128)(2,1)S(1)} copy-done((bf16[4,128,1024]{2,1,0:T(8,128)(2,1)S(1)}, bf16[4,128,1024]{2,1,0:T(8,128)(2,1)}, u32[]{:S(2)}) %copy-start) | copy-done | bytes 1048600
  13.7 0.0 copy-start.1
  13.7 1.0 %copy-done.1 = bf16[256,1024]{1,0:T(8,128)(2,1)S(1)} copy-done((bf16[256,1024]{1,0:T(8,128)(2,1)S(1)}, bf16[256,1024]{1,0:T(8,128)(2,1)}, u32[]{:S(2)}) %copy-start.1) | copy-done | bytes 524312
  14.7 0.0 copy-start.3
  14.7 0.7 copy-done.3
  15.4 0.0 copy-start.4
  15.4 0.7 copy-done.4
  16.1 0.0 copy-start.2
  16.1 0.0 copy-start.5
  16.1 5.3 %attend_own.1 = (bf16[256,128]{1,0:T(8,128)(2,1)S(1)}, s32[32,128]{1,0:T(8,128)S(1)}, f32[2,8,128]{2,1,0:T(8,128)S(1)}, f32[9,256,256]{2,1,0:T(8,128)S(1)}, f32[9,256,128]{2,1,0:T(8,128)S(1)}) custom-call(s32[1]{0:T(128)} %bitcast.here_ref, s32[32]{0:T(128)S(1)} %copy-done.4, s32[4,128]{1,0:T(4,128)S(1)} %copy-done.3, bf16[256,1024]{1,0:T(8,128)(2,1)S(1)} %copy-done.1, ...), custom_call_target="tpu_custom_call" | custom-call | flops 2415919104 | bytes 131072 | tf_op jit(solution)/shard_map/attend_own/pallas_call | solution.py:317
  21.4 0.0 collective-permute-done.rest_0_
  21.4 5.4 %collective-permute-start.1 = (bf16[1024,128]{1,0:T(8,128)(2,1)S(1)}, bf16[1024,128]{1,0:T(8,128)(2,1)S(1)}, u32[]{:S(2)}, u32[]{:S(2)}) collective-permute-start(bf16[1024,128]{1,0:T(8,128)(2,1)S(1)} %pad_maximum_fusion.rest_1_), channel_id=1, source_target_pairs={{0,224},{32,0},{64,32},{96,64},{128,96},{160,128},{192,160},{224,1... | collective-permute-start | bytes 786440 | tf_op jit(solution)/shard_map/ppermute | solution.py:279
  26.8 1.9 %collective-permute-start.2 = (bf16[1024,128]{1,0:T(8,128)(2,1)S(1)}, bf16[1024,128]{1,0:T(8,128)(2,1)S(1)}, u32[]{:S(2)}, u32[]{:S(2)}) collective-permute-start(bf16[1024,128]{1,0:T(8,128)(2,1)S(1)} %pad_maximum_fusion.rest_1_), channel_id=1, source_target_pairs={{0,32},{32,64},{64,96},{96,128},{128,160},{160,192},{192,224},{224... | collective-permute-start | bytes 786440 | tf_op jit(solution)/shard_map/ppermute | solution.py:279
  28.7 0.0 copy-done.2
  28.7 0.0 copy-done.5
  28.8 5.3 %attend_other.1 = (f32[2,8,128]{2,1,0:T(8,128)S(1)}, f32[9,256,256]{2,1,0:T(8,128)S(1)}, f32[9,256,128]{2,1,0:T(8,128)S(1)}) custom-call(s32[1]{0:T(128)} %bitcast.here_ref, s32[32]{0:T(128)S(1)} %copy-done.5, bf16[256,1024]{1,0:T(8,128)(2,1)S(1)} %copy-done.2, bf16[256,128]{1,0:T(8,128)(2,1)S(1)} %get-tuple-element.21.dec_query_ref, ...), custom_call_target="tpu_custom_call" | custom-call | flops 9663676416 | bytes 524288 | tf_op jit(solution)/shard_map/attend_other/pallas_call | solution.py:330
  34.0 0.0 collective-permute-done.1.rest_0_.rest_2_
  34.0 5.1 %collective-permute-start.3 = (bf16[1024,128]{1,0:T(8,128)(2,1)S(1)}, bf16[1024,128]{1,0:T(8,128)(2,1)S(1)}, u32[]{:S(2)}, u32[]{:S(2)}) collective-permute-start(bf16[1024,128]{1,0:T(8,128)(2,1)S(1)} %collective-permute-done.1.rest_0_.rest_2_), channel_id=1, source_target_pairs={{0,224},{32,0},{64,32},{96,64},{128,96},{160,128},{192,160},{224,1... | collective-permute-start | bytes 786440 | tf_op jit(solution)/shard_map/ppermute | solution.py:279
  39.2 0.0 collective-permute-done.2.rest_1_.rest_3_
  39.2 1.9 %collective-permute-start.4 = (bf16[1024,128]{1,0:T(8,128)(2,1)S(1)}, bf16[1024,128]{1,0:T(8,128)(2,1)S(1)}, u32[]{:S(2)}, u32[]{:S(2)}) collective-permute-start(bf16[1024,128]{1,0:T(8,128)(2,1)S(1)} %collective-permute-done.2.rest_1_.rest_3_), channel_id=1, source_target_pairs={{0,32},{32,64},{64,96},{96,128},{128,160},{160,192},{192,224},{224... | collective-permute-start | bytes 786440 | tf_op jit(solution)/shard_map/ppermute | solution.py:279
  41.1 9.8 %attend_0.1 = (f32[2,8,128]{2,1,0:T(8,128)S(1)}, f32[9,256,256]{2,1,0:T(8,128)S(1)}, f32[9,256,128]{2,1,0:T(8,128)S(1)}) custom-call(s32[1]{0:T(128)} %bitcast.here_ref, s32[32]{0:T(128)S(1)} %copy-done.5, bf16[256,1024]{1,0:T(8,128)(2,1)S(1)} %copy-done.2, bf16[256,128]{1,0:T(8,128)(2,1)S(1)} %get-tuple-element.21.dec_query_ref, ...), custom_call_target="tpu_custom_call" | custom-call | flops 9663676416 | bytes 524288 | tf_op jit(solution)/shard_map/attend_0/pallas_call | solution.py:330
  51.0 0.0 collective-permute-done.3.rest_0_.rest_4_
  51.0 5.1 %collective-permute-start.5 = (bf16[1024,128]{1,0:T(8,128)(2,1)S(1)}, bf16[1024,128]{1,0:T(8,128)(2,1)S(1)}, u32[]{:S(2)}, u32[]{:S(2)}) collective-permute-start(bf16[1024,128]{1,0:T(8,128)(2,1)S(1)} %collective-permute-done.3.rest_0_.rest_4_), channel_id=1, source_target_pairs={{0,224},{32,0},{64,32},{96,64},{128,96},{160,128},{192,160},{224,1... | collective-permute-start | bytes 786440 | tf_op jit(solution)/shard_map/ppermute | solution.py:279
  56.1 0.0 collective-permute-done.4.rest_1_.rest_5_
  56.1 1.9 %collective-permute-start.6 = (bf16[1024,128]{1,0:T(8,128)(2,1)S(1)}, bf16[1024,128]{1,0:T(8,128)(2,1)S(1)}, u32[]{:S(2)}, u32[]{:S(2)}) collective-permute-start(bf16[1024,128]{1,0:T(8,128)(2,1)S(1)} %collective-permute-done.4.rest_1_.rest_5_), channel_id=1, source_target_pairs={{0,32},{32,64},{64,96},{96,128},{128,160},{160,192},{192,224},{224... | collective-permute-start | bytes 786440 | tf_op jit(solution)/shard_map/ppermute | solution.py:279
  58.0 9.9 %attend_1.1 = (f32[2,8,128]{2,1,0:T(8,128)S(1)}, f32[9,256,256]{2,1,0:T(8,128)S(1)}, f32[9,256,128]{2,1,0:T(8,128)S(1)}) custom-call(s32[1]{0:T(128)} %bitcast.here_ref, s32[32]{0:T(128)S(1)} %copy-done.5, bf16[256,1024]{1,0:T(8,128)(2,1)S(1)} %copy-done.2, bf16[256,128]{1,0:T(8,128)(2,1)S(1)} %get-tuple-element.21.dec_query_ref, ...), custom_call_target="tpu_custom_call" | custom-call | flops 9663676416 | bytes 524288 | tf_op jit(solution)/shard_map/attend_1/pallas_call | solution.py:330
  68.0 0.0 collective-permute-done.5.rest_0_.rest_6_
  68.0 5.3 %collective-permute-start.7 = (bf16[1024,128]{1,0:T(8,128)(2,1)S(1)}, bf16[1024,128]{1,0:T(8,128)(2,1)S(1)}, u32[]{:S(2)}, u32[]{:S(2)}) collective-permute-start(bf16[1024,128]{1,0:T(8,128)(2,1)S(1)} %collective-permute-done.5.rest_0_.rest_6_), channel_id=1, source_target_pairs={{0,224},{32,0},{64,32},{96,64},{128,96},{160,128},{192,160},{224,1... | collective-permute-start | bytes 786440 | tf_op jit(solution)/shard_map/ppermute | solution.py:279
  73.3 0.0 collective-permute-done.6.rest_1_.rest_7_
  73.3 0.0 copy-start.6
  73.3 9.8 %attend_2.1 = (f32[2,8,128]{2,1,0:T(8,128)S(1)}, f32[9,256,256]{2,1,0:T(8,128)S(1)}, f32[9,256,128]{2,1,0:T(8,128)S(1)}) custom-call(s32[1]{0:T(128)} %bitcast.here_ref, s32[32]{0:T(128)S(1)} %copy-done.5, bf16[256,1024]{1,0:T(8,128)(2,1)S(1)} %copy-done.2, bf16[256,128]{1,0:T(8,128)(2,1)S(1)} %get-tuple-element.21.dec_query_ref, ...), custom_call_target="tpu_custom_call" | custom-call | flops 9663676416 | bytes 524288 | tf_op jit(solution)/shard_map/attend_2/pallas_call | solution.py:330
  83.1 0.0 collective-permute-done.7.rest_0_.rest_8_
  83.2 0.0 copy-done.6
  83.2 8.9 %attend_last.1 = (bf16[256,1024]{1,0:T(8,128)(2,1)}, bf16[256,128]{1,0:T(8,128)(2,1)}, bf16[256,128]{1,0:T(8,128)(2,1)}, bf16[4,8,1024]{2,1,0:T(8,128)(2,1)}) custom-call(s32[1]{0:T(128)} %bitcast.here_ref, s32[32]{0:T(128)S(1)} %copy-done.5, s32[16]{0:T(128)S(1)} %copy-done.6, bf16[256,1024]{1,0:T(8,128)(2,1)S(1)} %copy-done.2, ...), custom_call_target="tpu_custom_call" | custom-call | flops 4831838208 | bytes 262144 | tf_op jit(solution)/shard_map/attend_last/pallas_call | solution.py:349
  (1 shorter events, 0.0 us)
Async XLA Ops:
  1.5 19.9 %collective-permute-start = (bf16[512,128]{1,0:T(8,128)(2,1)S(1)}, bf16[512,128]{1,0:T(8,128)(2,1)S(1)}, u32[]{:S(2)}, u32[]{:S(2)}) collective-permute-start(bf16[512,128]{1,0:T(8,128)(2,1)S(1)} %pack.1.pairs_ref), channel_id=1, source_target_pairs={{0,256},{32,288},{64,320},{96,352},{128,384},{160,416},{192,448},{... | collective-permute-start | bytes 393224 | tf_op jit(solution)/shard_map/ppermute | solution.py:290
  12.5 1.2 %copy-start = (bf16[4,128,1024]{2,1,0:T(8,128)(2,1)S(1)}, bf16[4,128,1024]{2,1,0:T(8,128)(2,1)}, u32[]{:S(2)}) copy-start(bf16[4,128,1024]{2,1,0:T(8,128)(2,1)} %dec_ref.1) | copy-start | bytes 3145732
  13.7 1.0 %copy-start.1 = (bf16[256,1024]{1,0:T(8,128)(2,1)S(1)}, bf16[256,1024]{1,0:T(8,128)(2,1)}, u32[]{:S(2)}) copy-start(bf16[256,1024]{1,0:T(8,128)(2,1)} %query_ref.11) | copy-start | bytes 1572868
  14.7 0.7 copy-start.3
  15.4 0.7 copy-start.4
  16.1 12.7 %copy-start.2 = (bf16[256,1024]{1,0:T(8,128)(2,1)S(1)}, bf16[256,1024]{1,0:T(8,128)(2,1)}, u32[]{:S(2)}) copy-start(bf16[256,1024]{1,0:T(8,128)(2,1)} %query_ref.11) | copy-start | bytes 1572868
  16.1 12.7 %copy-start.5 = (s32[32]{0:T(128)S(1)}, s32[32]{0:T(128)}, u32[]{:S(2)}) copy-start(s32[32]{0:T(128)} %order_ref.11) | copy-start | bytes 388
  21.4 12.6 %collective-permute-start.1 = (bf16[1024,128]{1,0:T(8,128)(2,1)S(1)}, bf16[1024,128]{1,0:T(8,128)(2,1)S(1)}, u32[]{:S(2)}, u32[]{:S(2)}) collective-permute-start(bf16[1024,128]{1,0:T(8,128)(2,1)S(1)} %pad_maximum_fusion.rest_1_), channel_id=1, source_target_pairs={{0,224},{32,0},{64,32},{96,64},{128,96},{160,128},{192,160},{224,1... | collective-permute-start | bytes 786440 | tf_op jit(solution)/shard_map/ppermute | solution.py:279
  26.8 12.4 %collective-permute-start.2 = (bf16[1024,128]{1,0:T(8,128)(2,1)S(1)}, bf16[1024,128]{1,0:T(8,128)(2,1)S(1)}, u32[]{:S(2)}, u32[]{:S(2)}) collective-permute-start(bf16[1024,128]{1,0:T(8,128)(2,1)S(1)} %pad_maximum_fusion.rest_1_), channel_id=1, source_target_pairs={{0,32},{32,64},{64,96},{96,128},{128,160},{160,192},{192,224},{224... | collective-permute-start | bytes 786440 | tf_op jit(solution)/shard_map/ppermute | solution.py:279
  34.0 16.9 %collective-permute-start.3 = (bf16[1024,128]{1,0:T(8,128)(2,1)S(1)}, bf16[1024,128]{1,0:T(8,128)(2,1)S(1)}, u32[]{:S(2)}, u32[]{:S(2)}) collective-permute-start(bf16[1024,128]{1,0:T(8,128)(2,1)S(1)} %collective-permute-done.1.rest_0_.rest_2_), channel_id=1, source_target_pairs={{0,224},{32,0},{64,32},{96,64},{128,96},{160,128},{192,160},{224,1... | collective-permute-start | bytes 786440 | tf_op jit(solution)/shard_map/ppermute | solution.py:279
  39.2 16.9 %collective-permute-start.4 = (bf16[1024,128]{1,0:T(8,128)(2,1)S(1)}, bf16[1024,128]{1,0:T(8,128)(2,1)S(1)}, u32[]{:S(2)}, u32[]{:S(2)}) collective-permute-start(bf16[1024,128]{1,0:T(8,128)(2,1)S(1)} %collective-permute-done.2.rest_1_.rest_3_), channel_id=1, source_target_pairs={{0,32},{32,64},{64,96},{96,128},{128,160},{160,192},{192,224},{224... | collective-permute-start | bytes 786440 | tf_op jit(solution)/shard_map/ppermute | solution.py:279
  51.0 17.0 %collective-permute-start.5 = (bf16[1024,128]{1,0:T(8,128)(2,1)S(1)}, bf16[1024,128]{1,0:T(8,128)(2,1)S(1)}, u32[]{:S(2)}, u32[]{:S(2)}) collective-permute-start(bf16[1024,128]{1,0:T(8,128)(2,1)S(1)} %collective-permute-done.3.rest_0_.rest_4_), channel_id=1, source_target_pairs={{0,224},{32,0},{64,32},{96,64},{128,96},{160,128},{192,160},{224,1... | collective-permute-start | bytes 786440 | tf_op jit(solution)/shard_map/ppermute | solution.py:279
  56.1 17.2 %collective-permute-start.6 = (bf16[1024,128]{1,0:T(8,128)(2,1)S(1)}, bf16[1024,128]{1,0:T(8,128)(2,1)S(1)}, u32[]{:S(2)}, u32[]{:S(2)}) collective-permute-start(bf16[1024,128]{1,0:T(8,128)(2,1)S(1)} %collective-permute-done.4.rest_1_.rest_5_), channel_id=1, source_target_pairs={{0,32},{32,64},{64,96},{96,128},{128,160},{160,192},{192,224},{224... | collective-permute-start | bytes 786440 | tf_op jit(solution)/shard_map/ppermute | solution.py:279
  68.0 15.2 %collective-permute-start.7 = (bf16[1024,128]{1,0:T(8,128)(2,1)S(1)}, bf16[1024,128]{1,0:T(8,128)(2,1)S(1)}, u32[]{:S(2)}, u32[]{:S(2)}) collective-permute-start(bf16[1024,128]{1,0:T(8,128)(2,1)S(1)} %collective-permute-done.5.rest_0_.rest_6_), channel_id=1, source_target_pairs={{0,224},{32,0},{64,32},{96,64},{128,96},{160,128},{192,160},{224,1... | collective-permute-start | bytes 786440 | tf_op jit(solution)/shard_map/ppermute | solution.py:279
  73.3 9.9 %copy-start.6 = (s32[16]{0:T(128)S(1)}, s32[16]{0:T(128)}, u32[]{:S(2)}) copy-start(s32[16]{0:T(128)} %owner_ref.1) | copy-start | bytes 196
